TPU v7x, 32 devices: a whole 2x2x4 slice. The times are simulated.
32 devices in a mesh: gx: 4 (over z), gy: 4 (over y, x), gz: 2 (over core).
Axes of the slice: x: 2, y: 2, z: 4, core: 2. Of those that a mesh axis runs over, the one named last changes fastest.
Arguments:
- populations: float32 [27, 16, 64, 256], P(None, 'gx', 'gy', 'gz'), as said below
- relax: float32 [27], replicated, may hold values from 0.8 to 1.9
- entry_point: int32 [32768], P(('gx', 'gy', 'gz')), may hold values from 0 to 3599, as said below
- entry_offset: int32 [3, 32768], P(None, ('gx', 'gy', 'gz')), may hold values from -3 to 127, as said below
- entry_weight: float32 [64, 32768], P(None, ('gx', 'gy', 'gz')), may hold values from 0 to 0.04
- entry_count: int32 [32], P(('gx', 'gy', 'gz')), may hold values from 128 to 1024, as said below
- turbine_owner: int32 [4], replicated, may hold values from 0 to 3, each once
- mode_shapes: bfloat16 [4, 2700, 512], P('gx'), may hold values from -0.25 to 0.25
- coupling: float32 [4, 512, 512], P('gx')
- modal_disp: float32 [4, 512], P('gx'), may hold values from -6 to 6
- modal_vel: float32 [4, 512], P('gx'), may hold values from -0.6 to 0.6
- rigid_vel: float32 [4, 3, 900], P('gx'), may hold values from -0.9 to 0.9
- drag_coef: float32 [4, 900], P('gx'), may hold values from 200 to 2000
Outputs:
- populations_out: float32 [27, 16, 64, 256], P(None, 'gx', 'gy', 'gz')
- body_force: float32 [3, 16, 64, 256], P(None, 'gx', 'gy', 'gz')
- modal_disp_new: float32 [4, 512], P('gx')
- modal_vel_new: float32 [4, 512], P('gx')
Inputs may be any that keep to these rules, and one draw needn't show every extreme that they name: `entry_point`: the live slots of one device name points of at most two turbines and at most 512 slots for each; a point id is turbine 900 + point. Live slots are the first entry_count of a device's list. `entry_offset`: row c lies from 1 - 4 to the brick's cells along dimension c less one (4, 16, 128 in turn), so every tile meets its brick. `turbine_owner`: each gx index owns exactly one turbine. All populations are positive.
All inputs are finite; a program needn't handle non-finite values.
Results may differ from a plain program's by a relative error of at most 0.0036.
Values sent between devices are 32-bit elements; how exact they have to be, the bound alone decides.
A program may use at most 64 MiB of HBM per device.

v0:
```python
import jax
import jax.numpy as jnp
import numpy as np
from jax import lax
from jax.sharding import PartitionSpec as P

TILE_SIDE = 4


highest = lax.Precision.HIGHEST
inflow_speed = 0.05
force_unit = 0.02
modal_step = 0.004


def padded_2(cells, sides, width):
    for axis, dim in sides:
        count = lax.axis_size(axis)
        head = lax.slice_in_dim(cells, 0, width, axis=dim)
        tail = lax.slice_in_dim(cells, cells.shape[dim] - width, cells.shape[dim], axis=dim)
        cells = jnp.concatenate(
            [
                lax.ppermute(tail, axis, [(i, (i + 1) % count) for i in range(count)]),
                cells,
                lax.ppermute(head, axis, [((i + 1) % count, i) for i in range(count)]),
            ],
            axis=dim,
        )
    return cells


def lattice_tables():
    steps_np = np.array([-1.0, 0.0, 1.0])
    along_x = np.repeat(steps_np, 9)
    along_y = np.tile(np.repeat(steps_np, 3), 3)
    along_z = np.tile(steps_np, 9)
    velocity_np = np.stack([along_x, along_y, along_z])
    squared = (along_x * along_x + along_y * along_y + along_z * along_z).astype(np.int64)
    weight_np = np.array([8.0 / 27.0, 2.0 / 27.0, 1.0 / 54.0, 1.0 / 216.0])[squared]
    vander = np.array([[1.0, 1.0, 1.0], [-1.0, 0.0, 1.0], [1.0, 0.0, 1.0]])
    inverse_one = np.array([[0.0, -0.5, 0.5], [1.0, 0.0, -1.0], [0.0, 0.5, 0.5]])
    moment_np = np.kron(np.kron(vander, vander), vander)
    inverse_np = np.kron(np.kron(inverse_one, inverse_one), inverse_one)
    return (velocity_np, weight_np, moment_np, inverse_np)


def collide(
    lattice_flat,
    momentum,
    density,
    lattice_force,
    relax,
    velocity_table,
    weight_table,
    moment_table,
    inverse_table,
):
    velocity = (momentum + 0.5 * lattice_force) / density
    along = jnp.dot(velocity_table.T, velocity, precision=highest)
    pushed = jnp.dot(velocity_table.T, lattice_force, precision=highest)
    square = jnp.sum(velocity * velocity, axis=0)
    dotted = jnp.sum(velocity * lattice_force, axis=0)
    weight_col = weight_table[:, None]
    equilibrium = weight_col * density * (1.0 + 3.0 * along + 4.5 * along * along - 1.5 * square)
    source = weight_col * (3.0 * (pushed - dotted) + 9.0 * along * pushed)
    relaxed = jnp.dot(inverse_table * relax[None, :], moment_table, precision=highest)
    kept = jnp.dot(inverse_table * (1.0 - 0.5 * relax)[None, :], moment_table, precision=highest)
    return (
        lattice_flat
        - jnp.dot(relaxed, lattice_flat - equilibrium, precision=highest)
        + jnp.dot(kept, source, precision=highest)
    )


def inflow_populations(velocity_table, weight_table):
    along = inflow_speed * velocity_table[0]
    return weight_table * (
        1.0 + 3.0 * along + 4.5 * along * along - 1.5 * inflow_speed * inflow_speed
    )


def set_rims(padded, fill_values, dim, at_low, at_high):
    extent = padded.shape[dim]
    ramp_index = jnp.arange(extent, dtype=jnp.int32)
    rim_mask = (ramp_index == 0) & at_low | (ramp_index == extent - 1) & at_high
    rim_shape = [1] * padded.ndim
    rim_shape[dim] = extent
    fill_shape = [fill_values.shape[0]] + [1] * (padded.ndim - 1)
    return jnp.where(rim_mask.reshape(rim_shape), fill_values.reshape(fill_shape), padded)


def axis_select(offset, extent):
    steps_tile = jnp.arange(TILE_SIDE, dtype=jnp.int32)
    ramp_index = jnp.arange(extent, dtype=jnp.int32)
    return (offset[None, None, :] + steps_tile[:, None, None] == ramp_index[None, :, None]).astype(
        jnp.float32
    )


def layer_select(offset, extent):
    steps_tile = jnp.arange(TILE_SIDE, dtype=jnp.int32)
    ramp_index = jnp.arange(extent, dtype=jnp.int32)
    return (offset[None, None, :] + steps_tile[None, :, None] == ramp_index[:, None, None]).astype(
        jnp.float32
    )


def one_hot_rows(index, extent):
    return (index[:, None] == jnp.arange(extent, dtype=jnp.int32)[None, :]).astype(jnp.float32)


def body(
    populations,
    relax,
    entry_point,
    entry_offset,
    entry_weight,
    entry_count,
    turbine_owner,
    mode_shapes,
    coupling,
    modal_disp,
    modal_vel,
    rigid_vel,
    drag_coef,
):
    velocity_np, weight_np, moment_np, inverse_np = lattice_tables()
    velocity_table = jnp.asarray(velocity_np, jnp.float32)
    weight_table = jnp.asarray(weight_np, jnp.float32)
    moment_table = jnp.asarray(moment_np, jnp.float32)
    inverse_table = jnp.asarray(inverse_np, jnp.float32)
    size_x = populations.shape[1]
    size_y = populations.shape[2]
    size_z = populations.shape[3]
    cell_count = size_x * size_y * size_z
    slab_count = lax.axis_size("gx")
    points = drag_coef.shape[1]
    capacity = entry_point.shape[0]
    lattice_flat = populations.reshape(27, cell_count)
    density = jnp.sum(lattice_flat, axis=0)
    momentum = jnp.dot(velocity_table, lattice_flat, precision=highest)
    raw_velocity = momentum / density
    is_live = jnp.arange(capacity, dtype=jnp.int32) < entry_count[0]
    tile_weight = jnp.where(is_live[None, :], entry_weight, 0.0)
    weight_grid = tile_weight.reshape(TILE_SIDE, TILE_SIDE, TILE_SIDE, capacity)
    select_x = axis_select(entry_offset[0], size_x)
    select_y = axis_select(entry_offset[1], size_y)
    select_z = layer_select(entry_offset[2], size_z).reshape(size_z, TILE_SIDE * capacity)
    kernel_xk = jnp.einsum("abcr,axr->xbcr", weight_grid, select_x, precision=highest)
    kernel_xy = jnp.einsum("xbcr,byr->xycr", kernel_xk, select_y, precision=highest)
    layer_values = jnp.dot(
        raw_velocity.reshape(3 * size_x * size_y, size_z), select_z, precision=highest
    ).reshape(3, size_x, size_y, TILE_SIDE, capacity)
    partial_value = jnp.sum(kernel_xy[None] * layer_values, axis=(1, 2, 3))
    turbine = entry_point // points
    point_local = entry_point % points
    slab_ids = jnp.arange(slab_count, dtype=jnp.int32)
    owner_slab = jnp.sum(
        jnp.where(turbine[:, None] == slab_ids[None, :], turbine_owner[None, :], 0), axis=1
    )
    owner_table = (owner_slab[:, None] == slab_ids[None, :]).astype(jnp.float32)
    point_table = one_hot_rows(point_local, points)
    by_owner = jnp.einsum("cr,rs->csr", partial_value, owner_table, precision=highest)
    dense_sums = jnp.einsum("csr,rj->csj", by_owner, point_table, precision=highest)
    own_sums = lax.psum_scatter(dense_sums, "gx", scatter_dimension=1, tiled=True)
    sample = lax.psum(own_sums, ("gy", "gz"))[:, 0, :]
    shapes = mode_shapes[0]
    elastic = jnp.dot(
        shapes, modal_vel[0].astype(jnp.bfloat16), preferred_element_type=jnp.float32
    ).reshape(3, points)
    relative = sample - rigid_vel[0] - elastic
    rel_speed = jnp.sqrt(jnp.sum(relative * relative, axis=0))
    blade_force = drag_coef[0][None, :] * rel_speed[None, :] * relative
    modal_force = jnp.dot(
        blade_force.reshape(3 * points).astype(jnp.bfloat16),
        shapes,
        preferred_element_type=jnp.float32,
    )
    stiff_term = jnp.dot(coupling[0], modal_disp[0], precision=highest)
    vel_new = modal_vel[0] + modal_step * (modal_force - stiff_term)
    disp_new = modal_disp[0] + modal_step * vel_new
    all_force = lax.all_gather(blade_force[:, None, :], "gx", axis=1, tiled=True)
    per_slab = jnp.einsum("csj,rj->csr", all_force, point_table, precision=highest)
    entry_force = jnp.einsum("csr,rs->cr", per_slab, owner_table, precision=highest)
    weighted = (kernel_xy[None] * entry_force[:, None, None, None, :]).reshape(
        3 * size_x * size_y, TILE_SIDE * capacity
    )
    spread = jnp.dot(weighted, select_z.T, precision=highest)
    body_force = -spread.reshape(3, size_x, size_y, size_z)
    collided = collide(
        lattice_flat,
        momentum,
        density,
        force_unit * body_force.reshape(3, cell_count),
        relax,
        velocity_table,
        weight_table,
        moment_table,
        inverse_table,
    ).reshape(27, size_x, size_y, size_z)
    inflow = inflow_populations(velocity_table, weight_table)
    low_y = lax.axis_index("gy") == 0
    high_y = lax.axis_index("gy") == lax.axis_size("gy") - 1
    low_z = lax.axis_index("gz") == 0
    high_z = lax.axis_index("gz") == lax.axis_size("gz") - 1
    extended = padded_2(collided, (("gx", 1), ("gy", 2), ("gz", 3)), 1)
    extended = set_rims(extended, inflow, 2, low_y, high_y)
    extended = set_rims(extended, inflow, 3, low_z, high_z)
    pieces = []
    for i in range(27):
        a = int(velocity_np[0, i])
        b = int(velocity_np[1, i])
        c = int(velocity_np[2, i])
        pieces.append(
            extended[i, 1 - a : 1 - a + size_x, 1 - b : 1 - b + size_y, 1 - c : 1 - c + size_z]
        )
    populations_out = jnp.stack(pieces)
    return (populations_out, body_force, disp_new[None, :], vel_new[None, :])


def solution(mesh):
    return jax.shard_map(
        body,
        mesh=mesh,
        in_specs=(
            P(None, "gx", "gy", "gz"),
            P(),
            P(("gx", "gy", "gz")),
            P(None, ("gx", "gy", "gz")),
            P(None, ("gx", "gy", "gz")),
            P(("gx", "gy", "gz")),
            P(),
            P("gx", None, None),
            P("gx", None, None),
            P("gx", None),
            P("gx", None),
            P("gx", None, None),
            P("gx", None),
        ),
        out_specs=(
            P(None, "gx", "gy", "gz"),
            P(None, "gx", "gy", "gz"),
            P("gx", None),
            P("gx", None),
        ),
        check_vma=False,
    )
```

profile of v0, /device:TPU:0, one launch (start us, length us, event | category | flops | bytes accessed | tf_op | source)
XLA Modules:
  0.0 172.7 jit_solution(14686521104279196693)
XLA Ops:
  0.7 0.8 fusion.110
  1.5 0.2 iota_add_fusion
  2.4 1.0 broadcast_select_fusion
  3.4 0.1 reshape.193
  3.4 6.3 %copy.38 = f32[4,4,4,1024]{2,0,1,3:T(4,128)} copy(f32[4,4,4,1024]{3,2,1,0:T(4,128)S(1)} %reshape.193) | data formatting | bytes 524288 | tf_op jit(solution)/shard_map/reshape | solution.py:145
  9.7 0.2 iota_add_fusion.1
  9.9 11.1 %convolution_bitcast_fusion = f32[4,4,4,1024]{2,0,1,3:T(4,128)S(1)} fusion(f32[4,4,4,1024]{2,0,1,3:T(4,128)} %copy.38, s32[4,1024]{0,1:T(8,128)S(1)} %iota_add_fusion), kind=kOutput, calls=%fused_computation.5 | convolution fusion | flops 3162112 | bytes 540672 | tf_op jit(solution)/shard_map/abcr,axr->xbcr/dot_general | solution.py:149
  21.0 16.6 %fusion.2 = f32[4,16,4,1024]{1,2,0,3:T(4,128)} fusion(f32[4,4,4,1024]{2,0,1,3:T(4,128)S(1)} %convolution_bitcast_fusion, s32[4,1024]{0,1:T(8,128)S(1)} %iota_add_fusion.1), kind=kOutput, calls=%fused_computation.4 | convolution fusion | flops 12648448 | bytes 1327104 | tf_op jit(solution)/shard_map/xbcr,byr->xycr/dot_general | solution.py:150
  37.6 7.8 %copy.41 = f32[4,16,4,1024]{3,1,2,0:T(8,128)} copy(f32[4,16,4,1024]{1,2,0,3:T(4,128)} %fusion.2) | data formatting | bytes 2097152 | tf_op jit(solution)/shard_map/xbcr,byr->xycr/transpose | solution.py:150
  45.4 6.8 %copy.40 = f32[4,16,4,1024]{3,2,1,0:T(4,128)S(1)} copy(f32[4,16,4,1024]{1,2,0,3:T(4,128)} %fusion.2) | data formatting | bytes 2097152 | tf_op jit(solution)/shard_map/xbcr,byr->xycr/transpose | solution.py:150
  52.3 0.1 reduce_sum.56
  52.4 0.1 pad.8
  52.5 0.6 copy.67
  53.1 0.6 fusion.111
  53.9 0.1 select_reduce_fusion
  54.0 2.3 %multiply_reduce_fusion = f32[3,1024]{1,0:T(4,128)S(1)} fusion(f32[4,16,4,1024]{3,1,2,0:T(8,128)S(1)} %copy-done.2, s32[4,1024]{1,0:T(4,128)S(1)} %get-tuple-element.60, f32[3,4,16,128,1]{3,2,1,0,4:T(8,128)S(1)} %bitcast.169), kind=kOutput, calls=%fused_computation.14 | convolution fusion | flops 1210053632 | bytes 1175552 | tf_op jit(solution)/shard_map/dot_general | solution.py:151
  56.2 1.8 %fusion.8 = f32[3,4,900]{2,1,0:T(4,128)S(1)} fusion(s32[1024]{0:T(1024)S(1)} %get-tuple-element.62, f32[1024,4]{0,1:T(4,128)S(1)} %fusion.89, f32[1024,3]{0,1:T(4,128)S(1)} %bitcast.186), kind=kOutput, calls=%fused_computation.9 | convolution fusion | flops 133644288 | bytes 75968 | tf_op jit(solution)/shard_map/csr,rj->csj/dot_general | solution.py:164
  58.0 21.2 %all-reduce = f32[3,4,900]{2,1,0:T(4,128)S(1)} all-reduce(f32[3,4,900]{2,1,0:T(4,128)S(1)} %fusion.8), channel_id=3, replica_groups=mesh['gx'=4,'gy'=4,'gz'=2] {'gx'}, use_global_device_ids=true, to_apply=%region_3.4.clone | all-reduce | flops 10800 | bytes 86400
  79.3 0.6 dynamic-slice
  79.8 0.7 constant_dynamic-slice_fusion
  80.5 22.3 %psum.7 = f32[3,900]{1,0:T(4,128)S(1)} all-reduce(f32[3,900]{1,0:T(4,128)S(1)} %bitcast.172), channel_id=1, replica_groups=mesh['gx'=4,'gy'=4,'gz'=2] {'gy','gz'}, use_global_device_ids=true, to_apply=%region_4.5 | all-reduce | flops 2700 | bytes 21600 | tf_op jit(solution)/shard_map/psum | solution.py:166
  102.9 3.4 %dot_general.76 = bf16[3,900,512]{2,1,0:T(8,128)(2,1)} reshape(bf16[1,2700,512]{2,1,0:T(8,128)(2,1)} %param.24) | data formatting | bytes 5529600 | tf_op jit(solution)/shard_map/dot_general | solution.py:168
  106.3 2.6 %fusion.94 = f32[1,3,900]{2,0,1:T(1,128)S(1)} fusion(bf16[3,900,512]{2,1,0:T(8,128)(2,1)} %dot_general.76, f32[1,512]{1,0:T(1,128)S(1)} %copy-done.7), kind=kOutput, calls=%fused_computation.114 | convolution fusion | flops 2765312 | bytes 2777648 | tf_op jit(solution)/shard_map/dot_general | solution.py:168
  109.0 13.1 %all-gather.1 = f32[4,900,3]{1,2,0:T(4,128)S(1)} all-gather(f32[1,900,3]{1,2,0:T(4,128)S(1)} %get-tuple-element.55), channel_id=2, replica_groups=mesh['gx'=4,'gy'=4,'gz'=2] {'gx'}, dimensions={0}, use_global_device_ids=true | all-gather | bytes 54000 | tf_op jit(solution)/shard_map/all_gather | solution.py:182
  122.2 0.1 reshape.197
  122.3 0.1 reshape.195
  122.5 1.3 fusion.41
  123.8 1.7 mul.188
  125.5 3.8 %broadcast_multiply_fusion.1 = (f32[3,4,16,128]{3,2,1,0:T(8,128)S(1)}, f32[3,4,16,128]{3,2,1,0:T(8,128)S(1)}, f32[3,4,16,128]{3,2,1,0:T(8,128)}) fusion(s32[4096]{0:T(1024)S(1)} %bitcast.176, f32[3,4096]{1,0:T(4,128)S(1)} %bitcast.171, f32[4,16,4096]{2,1,0:T(8,128)} %mul.188), kind=kOutput, calls=%fused_computation.80 | convolution fusion | flops 1209344000 | bytes 1409024 | tf_op jit(solution)/shard_map/dot_general | solution.py:188
  129.3 1.1 fusion.74
  130.4 0.3 fusion.77
  130.7 1.1 fusion.112
  131.8 0.1 fusion.87
  131.9 0.1 fusion.85
  132.1 1.3 convolution_subtract_fusion
  133.4 1.1 convolution_add_fusion
  134.5 0.2 copy.73
  134.8 0.1 copy.91
  135.0 0.8 copy.92
  135.8 3.8 %collective-permute-start.1 = (f32[27,1,16,128]{3,0,2,1:T(8,128)}, f32[27,1,16,128]{3,0,2,1:T(8,128)}, u32[]{:S(2)}, u32[]{:S(2)}) collective-permute-start(f32[27,1,16,128]{3,0,2,1:T(8,128)} %copy.92), channel_id=1, source_target_pairs={{8,0},{16,8},{24,16},{0,24},{9,1},{17,9},{25,17},{1,25},{10,2},{18... | collective-permute-start | bytes 663560 | tf_op jit(solution)/shard_map/ppermute | solution.py:25
  139.6 0.1 reshape.208
  139.7 2.2 %fusion.13 = f32[1,512]{1,0:T(1,128)S(1)} fusion(bf16[2700,1]{0,1:T(2,128)(2,1)S(1)} %reshape.208, bf16[1,2700,512]{2,1,0:T(8,128)(2,1)} %param.24), kind=kOutput, calls=%fused_computation.15 | convolution fusion | flops 2764800 | bytes 2772248 | tf_op jit(solution)/shard_map/dot_general | solution.py:174
  141.9 1.0 fusion.49
  142.9 0.6 multiply_add_fusion
  143.5 1.0 constant_dynamic-update-slice_fusion.1
  144.5 0.5 copy_dynamic-update-slice_fusion
  145.0 0.2 collective-permute-done.1
  145.3 1.0 constant_dynamic-update-slice_fusion
  146.3 1.7 %collective-permute-start.2 = (f32[27,6,1,128]{3,0,2,1:T(8,128)S(1)}, f32[27,6,1,128]{3,0,2,1:T(8,128)S(1)}, u32[]{:S(2)}, u32[]{:S(2)}) collective-permute-start(f32[27,6,1,128]{3,0,2,1:T(8,128)S(1)} %get-tuple-element.48), channel_id=1, source_target_pairs={{0,2},{2,4},{4,6},{6,0},{1,3},{3,5},{5,7},{7,1},{8,10},{10,12},{12... | collective-permute-start | bytes 248840 | tf_op jit(solution)/shard_map/ppermute | solution.py:23
  148.0 1.2 collective-permute-start.3
  149.2 2.6 %collective-permute-done.2 = f32[27,6,1,128]{3,0,2,1:T(8,128)S(1)} collective-permute-done((f32[27,6,1,128]{3,0,2,1:T(8,128)S(1)}, f32[27,6,1,128]{3,0,2,1:T(8,128)S(1)}, u32[]{:S(2)}, u32[]{:S(2)}) %collective-permute-start.2) | collective-permute-done | bytes 82976 | tf_op jit(solution)/shard_map/ppermute | solution.py:23
  151.8 1.1 collective-permute-done.3
  152.9 0.2 pad_maximum_fusion
  153.1 2.4 %fusion.107 = (f32[27,6,18,1]{3,0,2,1:T(8,128)}, f32[27,6,18,1]{3,0,2,1:T(8,128)}) fusion(f32[27,6,18,128]{3,0,2,1:T(8,128)S(1)} %pad_maximum_fusion), kind=kLoop, calls=%fused_computation.131 | loop fusion | bytes 46656 | tf_op jit(solution)/shard_map/slice | solution.py:20
  155.5 2.4 %copy.46 = f32[27,6,18,1]{0,2,3,1:T(8,128)S(1)} copy(f32[27,6,18,1]{3,0,2,1:T(8,128)} %get-tuple-element.46) | data formatting | bytes 23328 | tf_op jit(solution)/shard_map/slice | solution.py:20
  157.9 2.4 %copy.47 = f32[27,6,18,1]{0,2,3,1:T(8,128)S(1)} copy(f32[27,6,18,1]{3,0,2,1:T(8,128)} %get-tuple-element.47) | data formatting | bytes 23328 | tf_op jit(solution)/shard_map/slice | solution.py:19
  160.4 0.5 collective-permute-start.5
  160.9 2.0 %copy.48 = f32[27,6,18,1]{3,0,2,1:T(8,128)} copy(f32[27,6,18,1]{0,2,3,1:T(8,128)S(1)} %collective-permute-done.4) | data formatting | bytes 23328 | tf_op jit(solution)/shard_map/ppermute | solution.py:23
  162.9 2.0 %copy.49 = f32[27,6,18,1]{3,0,2,1:T(8,128)} copy(f32[27,6,18,1]{0,2,3,1:T(8,128)S(1)} %collective-permute-done.5) | data formatting | bytes 23328 | tf_op jit(solution)/shard_map/ppermute | solution.py:25
  164.9 3.5 %fusion.10 = f32[27,6,18,130]{3,0,2,1:T(8,128)S(1)} fusion(f32[27,6,18,1]{3,0,2,1:T(8,128)} %copy.49, f32[27,6,1,128]{3,0,2,1:T(8,128)S(1)} %collective-permute-done.3, f32[27,6,16,128]{3,0,2,1:T(8,128)S(1)} %constant_dynamic-update-slice_fusion, f32[27,6,1,128]{3,0,2,1:T(8,128)S(1)} %collective-permute-done.2, f32[27,6,18,1]{3,0,2,1:T(8,128)} %copy.48, ...), kind=kLoop, calls=%fused_computation.11 | loop fusion | flops 2274480 | bytes 3032896 | tf_op jit(solution)/shard_map/jit(_where)/select_n | solution.py:89
  168.4 1.0 fusion.105
  169.4 0.5 fusion.106
  169.9 1.4 stack.3
  171.2 1.4 copy.50
  (59 shorter events, 0.6 us)
Async XLA Ops:
  0.6 141.3 %copy-start = (f32[1,512,512]{2,1,0:T(8,128)S(1)}, f32[1,512,512]{2,1,0:T(8,128)}, u32[]{:S(2)}) copy-start(f32[1,512,512]{2,1,0:T(8,128)} %param.25) | copy-start | bytes 3145732
  45.4 6.8 %copy-start.1 = (f32[27,4,16,128]{3,2,1,0:T(8,128)S(1)}, f32[27,4,16,128]{3,2,1,0:T(8,128)}, u32[]{:S(2)}) copy-start(f32[27,4,16,128]{3,2,1,0:T(8,128)} %param.17) | copy-start | bytes 2654212
  52.3 0.8 copy-start.5
  52.3 1.5 copy-start.9
  52.3 1.5 copy-start.14
  52.4 1.6 copy-start.2
  53.1 26.1 %copy-start.15 = (u32[32]{0:T(128)S(1)}, u32[32]{0:T(128)}, u32[]{:S(2)}) copy-start(u32[32]{0:T(128)} %constant.103) | copy-start | bytes 388
  102.9 3.4 %copy-start.7 = (f32[1,512]{1,0:T(1,128)S(1)}, f32[1,512]{1,0:T(1,128)}, u32[]{:S(2)}) copy-start(f32[1,512]{1,0:T(1,128)} %param.27) | copy-start | bytes 6148
  106.3 2.6 %copy-start.6 = (f32[1,3,900]{2,0,1:T(1,128)S(1)}, f32[1,3,900]{2,0,1:T(1,128)}, u32[]{:S(2)}) copy-start(f32[1,3,900]{2,0,1:T(1,128)} %param.28) | copy-start | bytes 32404
  106.3 2.7 %copy-start.10 = (f32[1,900]{1,0:T(1,128)S(1)}, f32[1,900]{1,0:T(1,128)}, u32[]{:S(2)}) copy-start(f32[1,900]{1,0:T(1,128)} %param.29) | copy-start | bytes 10804
  125.5 6.3 %copy-start.12 = (f32[27]{0:T(128)S(1)}, f32[27]{0:T(128)}, u32[]{:S(2)}) copy-start(f32[27]{0:T(128)} %param.18) | copy-start | bytes 328
  125.5 6.3 %copy-start.3 = (f32[27,27]{1,0:T(8,128)S(1)}, f32[27,27]{1,0:T(8,128)}, u32[]{:S(2)}) copy-start(f32[27,27]{1,0:T(8,128)} %constant.81.clone) | copy-start | bytes 8752
  125.5 6.3 %copy-start.4 = (f32[27,27]{1,0:T(8,128)S(1)}, f32[27,27]{1,0:T(8,128)}, u32[]{:S(2)}) copy-start(f32[27,27]{1,0:T(8,128)} %constant.82.clone) | copy-start | bytes 8752
  125.5 6.6 %copy-start.11 = (f32[27]{0:T(128)S(1)}, f32[27]{0:T(128)}, u32[]{:S(2)}) copy-start(f32[27]{0:T(128)} %constant.80.clone) | copy-start | bytes 328
  134.8 7.1 %copy-start.8 = (f32[1,512]{1,0:T(1,128)S(1)}, f32[1,512]{1,0:T(1,128)}, u32[]{:S(2)}) copy-start(f32[1,512]{1,0:T(1,128)} %param.26) | copy-start | bytes 6148
  134.9 8.6 %collective-permute-start = (f32[27,1,16,128]{3,0,2,1:T(8,128)S(1)}, f32[27,1,16,128]{3,0,2,1:T(8,128)}, u32[]{:S(2)}, u32[]{:S(2)}) collective-permute-start(f32[27,1,16,128]{3,0,2,1:T(8,128)S(1)} %copy.91), channel_id=1, source_target_pairs={{0,8},{8,16},{16,24},{24,0},{1,9},{9,17},{17,25},{25,1},{2,10},{10... | collective-permute-start | bytes 663560 | tf_op jit(solution)/shard_map/ppermute | solution.py:23
  135.8 9.5 %collective-permute-start.1 = (f32[27,1,16,128]{3,0,2,1:T(8,128)}, f32[27,1,16,128]{3,0,2,1:T(8,128)}, u32[]{:S(2)}, u32[]{:S(2)}) collective-permute-start(f32[27,1,16,128]{3,0,2,1:T(8,128)} %copy.92), channel_id=1, source_target_pairs={{8,0},{16,8},{24,16},{0,24},{9,1},{17,9},{25,17},{1,25},{10,2},{18... | collective-permute-start | bytes 663560 | tf_op jit(solution)/shard_map/ppermute | solution.py:25
  146.3 5.6 %collective-permute-start.2 = (f32[27,6,1,128]{3,0,2,1:T(8,128)S(1)}, f32[27,6,1,128]{3,0,2,1:T(8,128)S(1)}, u32[]{:S(2)}, u32[]{:S(2)}) collective-permute-start(f32[27,6,1,128]{3,0,2,1:T(8,128)S(1)} %get-tuple-element.48), channel_id=1, source_target_pairs={{0,2},{2,4},{4,6},{6,0},{1,3},{3,5},{5,7},{7,1},{8,10},{10,12},{12... | collective-permute-start | bytes 248840 | tf_op jit(solution)/shard_map/ppermute | solution.py:23
  148.0 4.9 %collective-permute-start.3 = (f32[27,6,1,128]{3,0,2,1:T(8,128)S(1)}, f32[27,6,1,128]{3,0,2,1:T(8,128)S(1)}, u32[]{:S(2)}, u32[]{:S(2)}) collective-permute-start(f32[27,6,1,128]{3,0,2,1:T(8,128)S(1)} %get-tuple-element.49), channel_id=1, source_target_pairs={{2,0},{4,2},{6,4},{0,6},{3,1},{5,3},{7,5},{1,7},{10,8},{12,10},{14... | collective-permute-start | bytes 248840 | tf_op jit(solution)/shard_map/ppermute | solution.py:25
  157.9 7.1 %copy-start.13 = (f32[27]{0:T(128)S(1)}, f32[27]{0:T(128)}, u32[]{:S(2)}) copy-start(f32[27]{0:T(128)} %constant.99) | copy-start | bytes 328
  157.9 3.0 %collective-permute-start.4 = (f32[27,6,18,1]{0,2,3,1:T(8,128)S(1)}, f32[27,6,18,1]{0,2,3,1:T(8,128)S(1)}, u32[]{:S(2)}, u32[]{:S(2)}) collective-permute-start(f32[27,6,18,1]{0,2,3,1:T(8,128)S(1)} %copy.46), channel_id=1, source_target_pairs={{0,1},{1,0},{2,3},{3,2},{4,5},{5,4},{6,7},{7,6},{8,9},{9,8},{10,11... | collective-permute-start | bytes 35000 | tf_op jit(solution)/shard_map/ppermute | solution.py:23
  160.4 2.6 %collective-permute-start.5 = (f32[27,6,18,1]{0,2,3,1:T(8,128)S(1)}, f32[27,6,18,1]{0,2,3,1:T(8,128)S(1)}, u32[]{:S(2)}, u32[]{:S(2)}) collective-permute-start(f32[27,6,18,1]{0,2,3,1:T(8,128)S(1)} %copy.47), channel_id=1, source_target_pairs={{1,0},{0,1},{3,2},{2,3},{5,4},{4,5},{7,6},{6,7},{9,8},{8,9},{11,10... | collective-permute-start | bytes 35000 | tf_op jit(solution)/shard_map/ppermute | solution.py:25
where the time goes:
time: 173 us
  blocking collectives  56.7 us (33%)
  local copies, waits for them, and re-layouts  48.5 us (28%)
  matrix products  48.1 us (28%)
  starting transfers between devices  7.43 us (4%)
  other arithmetic  6.19 us (4%)
  waiting for transfers between devices  3.93 us (2%)
  between operations  1.85 us (1%)
    psum x1, blocking collectives, body(): sample = lax.psum(own_sums, ('gy', 'gz'))[:, 0, :]  22.3 us
    unnamed x1, blocking collectives  21.2 us
    dot_general x1, matrix products, body(): jnp.einsum('xbcr,byr->xycr', kernel_xk, select_y, precision=highest)  16.6 us
    transpose x2, local copies, waits for them, and re-layouts, body(): jnp.einsum('xbcr,byr->xycr', kernel_xk, select_y, precision=highest)  14.7 us
    all_gather x1, blocking collectives, body(): lax.all_gather(blade_force[:, None, :], 'gx', axis=1, tiled=True)  13.1 us
    dot_general x1, matrix products, body(): jnp.einsum('abcr,axr->xbcr', weight_grid, select_x, precision=highest)  11.1 us
    reshape x2, local copies, waits for them, and re-layouts, body(): weight_grid = tile_weight.reshape(TILE_SIDE, TILE_SIDE, TILE_SIDE, capacity)  6.33 us
    unnamed x49, local copies, waits for them, and re-layouts  6.25 us
  transfers between devices with their start and end apart: 6, of which 3 were waited for; matrix products, arithmetic and copies ran while one was open for 6% of the time, Pallas kernels for 0%

commit v1 on v0

v1 whole, which is shorter than its diff:
```python
import functools

import jax
import jax.numpy as jnp
import numpy as np
from jax import lax
from jax.experimental import pallas as pl
from jax.experimental.pallas import tpu as pltpu
from jax.sharding import PartitionSpec as P

TILE_SIDE = 4
LANES = 128
CHUNK = 256
MESH = pl.DeviceIdType.MESH

highest = lax.Precision.HIGHEST
inflow_speed = 0.05
force_unit = 0.02
modal_step = 0.004

NT = (((1,), (1,)), ((), ()))
NN = (((1,), (0,)), ((), ()))


def inflow_values():
    steps = (-1.0, 0.0, 1.0)
    values = []
    for a in steps:
        for b in steps:
            for c in steps:
                weight = (8.0 / 27.0, 2.0 / 27.0, 1.0 / 54.0, 1.0 / 216.0)[
                    int(a * a + b * b + c * c)
                ]
                along = inflow_speed * a
                values.append(
                    weight
                    * (1.0 + 3.0 * along + 4.5 * along * along - 1.5 * inflow_speed * inflow_speed)
                )
    return [float(np.float32(v)) for v in values]


def transform(values, one):
    values = list(values)
    for stride in (9, 3, 1):
        for base in range(27):
            if base // stride % 3 == 0:
                spots = (base, base + stride, base + 2 * stride)
                for spot, value in zip(spots, one(*(values[s] for s in spots))):
                    values[spot] = value
    return values


def to_moments(low, mid, high):
    both = low + high
    return both + mid, high - low, both


def from_moments(zeroth, first, second):
    return 0.5 * (second - first), zeroth - second, 0.5 * (first + second)


def halves(value):
    high = value.astype(jnp.bfloat16)
    return high, (value - high.astype(jnp.float32)).astype(jnp.bfloat16)


def kernel(
    sizes,
    pops,
    relax,
    point_in,
    offset_in,
    weight_in,
    count_in,
    owner_in,
    shapes_hbm,
    stiff_in,
    disp_in,
    vel_in,
    aux_in,
    pops_out,
    force_out,
    disp_out,
    vel_out,
    shapes,
    moments,
    cells,
    raw_pair,
    pick_z,
    kern_xy,
    pick_low,
    dense,
    dense_in,
    slab_sum,
    slab_in,
    aux,
    aux_all,
    blade,
    blade_all,
    erow,
    spread,
    z_send,
    z_in,
    y_send,
    y_in,
    x_in,
    copy_sem,
    send_sem,
    recv_sem,
):
    slabs, columns, layers, points, size_x, size_y = sizes
    ranks = columns * layers
    padded = blade.shape[0] // 3
    rows = 3 * padded
    capacity = point_in.shape[1]
    plane = size_x * size_y
    gx = lax.axis_index("gx")
    gy = lax.axis_index("gy")
    gz = lax.axis_index("gz")
    rank = gy * layers + gz
    inflow = inflow_values()

    load_shapes = pltpu.make_async_copy(shapes_hbm, shapes, copy_sem)
    load_shapes.start()

    def slab_peer(step):
        return lax.rem(rank + step, ranks)

    def slab_id(other):
        return (gx, lax.div(other, layers), lax.rem(other, layers))

    def far_id(step):
        return (lax.rem(gx + step, slabs), gy, gz)

    barrier = pltpu.get_barrier_semaphore()
    for step in range(1, slabs):
        pl.semaphore_signal(barrier, inc=1, device_id=far_id(step), device_id_type=MESH)
    for step in range(1, ranks):
        pl.semaphore_signal(
            barrier, inc=1, device_id=slab_id(slab_peer(step)), device_id_type=MESH
        )

    used = [0]
    started = []

    def send(src, dst, device):
        copy = pltpu.make_async_remote_copy(
            src_ref=src,
            dst_ref=dst,
            send_sem=send_sem.at[used[0]],
            recv_sem=recv_sem.at[used[0]],
            device_id=device,
            device_id_type=MESH,
        )
        used[0] += 1
        copy.start()
        started.append(copy)
        return copy

    def moments_of(step, _):
        part = pl.ds(pl.multiple_of(step * 8, 8), 8)
        values = transform([pops[i, part, :] for i in range(27)], to_moments)
        for m in range(27):
            moments[m, part, :] = values[m]
        inverse = 1.0 / values[0]
        for c, m in enumerate((9, 3, 1)):
            raw = values[m] * inverse
            spot = pl.ds(pl.multiple_of(step * 8 + c * plane, 8), 8)
            spread[spot, :] = raw
        return 0

    lax.fori_loop(0, plane // 8, moments_of, 0)
    raw_high, raw_low = halves(spread[...])
    raw_pair[:, :LANES] = raw_high
    raw_pair[:, LANES:] = raw_low

    load_shapes.wait()
    vel8 = jnp.broadcast_to(vel_in[...], (8, vel_in.shape[1])).astype(jnp.bfloat16)
    erow[...] = jnp.zeros_like(erow)
    erow[:, : 3 * points] = lax.dot_general(
        vel8, shapes[...], NT, preferred_element_type=jnp.float32
    )
    width = erow.shape[1]
    line = erow[...]
    shifted = [
        line if c == 0 else pltpu.roll(line, width - c * points, 1) for c in range(3)
    ]
    row8 = lax.broadcasted_iota(jnp.int32, (8, LANES), 0)
    lane8 = lax.broadcasted_iota(jnp.int32, (8, LANES), 1)
    for jh in range(8):
        spot = slice(jh * LANES, (jh + 1) * LANES)
        both = jnp.where(
            row8 == 0,
            shifted[0][:, spot],
            jnp.where(row8 == 1, shifted[1][:, spot], shifted[2][:, spot]),
        )
        inside = (row8 < 3) & (lane8 + jh * LANES < points)
        aux[jh] = aux_in[jh] + jnp.where(inside, both, 0.0)
    pl.semaphore_wait(barrier, slabs - 1 + ranks - 1)
    aux_copies = [
        send(aux.at[rank], aux_all.at[gx], far_id(step)) for step in range(1, slabs)
    ]
    aux_all[gx] = aux[rank]

    dense[...] = jnp.zeros_like(dense)
    count = count_in[0]
    iota_y = lax.broadcasted_iota(jnp.int32, (size_y, CHUNK), 0)
    iota_z = lax.broadcasted_iota(jnp.int32, (LANES, CHUNK), 0)
    iota_s = lax.broadcasted_iota(jnp.int32, (padded, CHUNK), 0)
    iota_r = lax.broadcasted_iota(jnp.int32, (1, CHUNK), 1)

    def slots_of(part):
        name = point_in[:, part]
        turbine = jnp.zeros_like(name)
        for t in range(1, slabs):
            turbine = turbine + jnp.where(name >= t * points, 1, 0)
        owner = jnp.zeros_like(name)
        for t in range(slabs):
            owner = owner + jnp.where(turbine == t, owner_in[t], 0)
        point = name - turbine * points
        high = lax.shift_right_logical(point, 7)
        masks = [(iota_s == owner) & (high == jh) for jh in range(8)]
        return point - high * LANES, masks

    def gather(step, _):
        base = pl.multiple_of(step * CHUNK, CHUNK)
        part = pl.ds(base, CHUNK)
        weight = jnp.where(iota_r + base < count, weight_in[:, part], 0.0)
        off_x = offset_in[0:1, part]
        off_y = offset_in[1:2, part]
        off_z = offset_in[2:3, part]
        at_y = [off_y + b == iota_y for b in range(TILE_SIDE)]
        by_x = []
        for x in range(size_x):
            value = jnp.zeros((16, CHUNK), jnp.float32)
            for a in range(TILE_SIDE):
                value = jnp.where(off_x + a == x, weight[16 * a : 16 * a + 16], value)
            by_x.append(value)
        total = [jnp.zeros((size_y, CHUNK), jnp.float32) for _ in range(3)]
        for c in range(TILE_SIDE):
            at_z = jnp.where(off_z + c == iota_z, 1.0, 0.0).astype(jnp.bfloat16)
            pick_z[c, :, part] = at_z
            layer = lax.dot_general(
                raw_pair[...],
                jnp.concatenate([at_z, at_z], axis=0),
                NN,
                preferred_element_type=jnp.float32,
            )
            for x in range(size_x):
                value = jnp.zeros((size_y, CHUNK), jnp.float32)
                for b in range(TILE_SIDE):
                    row = 4 * b + c
                    value = jnp.where(at_y[b], by_x[x][row : row + 1], value)
                kern_xy[c, x * size_y : (x + 1) * size_y, part] = value
                for d in range(3):
                    first = d * plane + x * size_y
                    total[d] = total[d] + value * layer[first : first + size_y]
        partial = [jnp.sum(t, axis=0, keepdims=True) for t in total]
        low, masks = slots_of(part)
        at_low = jnp.where(low == iota_z, 1.0, 0.0).astype(jnp.bfloat16)
        pick_low[:, part] = at_low
        placed = jnp.concatenate(
            [jnp.where(masks[jh], partial[d], 0.0) for jh in range(8) for d in range(3)], axis=0
        )
        high_part, low_part = halves(placed)
        dense[...] += (
            lax.dot_general(high_part, at_low, NT, preferred_element_type=jnp.float32)
            + lax.dot_general(low_part, at_low, NT, preferred_element_type=jnp.float32)
        ).reshape(8, rows, LANES)
        return 0

    lax.fori_loop(0, capacity // CHUNK, gather, 0)

    first_copies = [
        send(dense.at[slab_peer(step)], dense_in.at[step - 1], slab_id(slab_peer(step)))
        for step in range(1, ranks)
    ]
    own = dense[rank]
    for step in range(1, ranks):
        first_copies[step - 1].wait_recv()
        own = own + dense_in[step - 1]
    slab_sum[...] = own
    second_copies = [
        send(slab_sum, slab_in.at[step - 1], far_id(step)) for step in range(1, slabs)
    ]
    for copy in aux_copies:
        copy.wait_recv()
    for step in range(1, slabs):
        second_copies[step - 1].wait_recv()
        own = own + slab_in[step - 1]

    blade[...] = jnp.zeros_like(blade)
    for s in range(slabs):
        here = aux_all[s]
        relative = [
            own[d * padded + s : d * padded + s + 1] - here[d : d + 1] for d in range(3)
        ]
        speed = jnp.sqrt(
            relative[0] * relative[0] + relative[1] * relative[1] + relative[2] * relative[2]
        )
        factor = here[3:4] * speed
        for d in range(3):
            spot = d * padded + s
            blade[spot : spot + 1, :] = factor * relative[d]
    blade_all[rank] = blade[...]
    third_copies = [
        send(blade, blade_all.at[rank], slab_id(slab_peer(step))) for step in range(1, ranks)
    ]
    for copy in third_copies:
        copy.wait_recv()

    blade_high, blade_low = halves(blade_all[...].reshape(8 * rows, LANES))
    blade_pair = jnp.concatenate([blade_high, blade_low], axis=1)
    spread[...] = jnp.zeros_like(spread)

    def scatter(step, _):
        part = pl.ds(pl.multiple_of(step * CHUNK, CHUNK), CHUNK)
        _, masks = slots_of(part)
        at_low = pick_low[:, part]
        found = lax.dot_general(
            blade_pair,
            jnp.concatenate([at_low, at_low], axis=0),
            NN,
            preferred_element_type=jnp.float32,
        )
        forces = []
        for d in range(3):
            value = jnp.zeros((padded, CHUNK), jnp.float32)
            for jh in range(8):
                first = jh * rows + d * padded
                value = jnp.where(masks[jh], found[first : first + padded], value)
            forces.append(jnp.sum(value, axis=0, keepdims=True))
        total = jnp.zeros(spread.shape, jnp.float32)
        for c in range(TILE_SIDE):
            kern = kern_xy[c, :, part]
            high_part, low_part = halves(
                jnp.concatenate([kern * forces[d] for d in range(3)], axis=0)
            )
            at_z = pick_z[c, :, part]
            total = total + (
                lax.dot_general(high_part, at_z, NT, preferred_element_type=jnp.float32)
                + lax.dot_general(low_part, at_z, NT, preferred_element_type=jnp.float32)
            )
        spread[...] += total
        return 0

    lax.fori_loop(0, capacity // CHUNK, scatter, 0)
    force_out[...] = -spread[...]

    def collide(step, _):
        part = pl.ds(pl.multiple_of(step * 8, 8), 8)
        density = moments[0, part, :]
        inverse = 1.0 / density
        force = [
            force_unit * force_out[pl.ds(pl.multiple_of(step * 8 + d * plane, 8), 8), :]
            for d in range(3)
        ]
        velocity = [
            (moments[m, part, :] + 0.5 * force[d]) * inverse for d, m in enumerate((9, 3, 1))
        ]
        pushed = [density * v for v in velocity]
        pairs = {}
        sources = {}
        for d in range(3):
            for e in range(d, 3):
                pairs[d, e] = pushed[d] * velocity[e]
                sources[d, e] = velocity[d] * force[e] + velocity[e] * force[d]
        values = []
        for m in range(27):
            powers = (m // 9, m // 3 % 3, m % 3)
            odd = [d for d in range(3) if powers[d] == 1]
            even = [d for d in range(3) if powers[d] == 2]
            scale = (1.0 / 3.0) ** len(even)
            source = None
            if len(odd) == 0:
                wanted = density * scale
                if even:
                    square = pairs[even[0], even[0]]
                    source = sources[even[0], even[0]]
                    for d in even[1:]:
                        square = square + pairs[d, d]
                        source = source + sources[d, d]
                    wanted = wanted + square * (3.0 * scale)
                    source = source * (3.0 * scale)
            elif len(odd) == 1:
                wanted = pushed[odd[0]] * scale
                source = force[odd[0]] * scale
            elif len(odd) == 2:
                wanted = pairs[odd[0], odd[1]] * scale
                source = sources[odd[0], odd[1]] * scale
            else:
                wanted = None
            rate = relax[m]
            here = moments[m, part, :]
            gap = here if wanted is None else here - wanted
            value = -rate * gap
            if source is not None:
                value = value + (1.0 - 0.5 * rate) * source
            values.append(value)
        values = transform(values, from_moments)
        for i in range(27):
            cells[i, part, :] = pops[i, part, :] + values[i]
        return 0

    lax.fori_loop(0, plane // 8, collide, 0)

    lane = lax.broadcasted_iota(jnp.int32, (plane, LANES), 1)
    at_bottom = gz == 0
    packed = jnp.zeros((plane, LANES), jnp.float32)
    for k in range(9):
        column = jnp.where(
            at_bottom,
            pltpu.roll(cells[3 * k + 2], k + 1, 1),
            cells[3 * k] if k == 0 else pltpu.roll(cells[3 * k], k, 1),
        )
        packed = jnp.where(lane == k, column, packed)
    z_send[...] = packed
    z_copy = send(z_send, z_in, (gx, gy, 1 - gz))

    pieces = []
    for d in range(3):
        chunks = [
            jnp.broadcast_to(blade_all[jh, pl.ds(d * padded + gx, 1), :], (8, LANES))
            for jh in range(8)
        ]
        chunks.append(jnp.zeros((8, width - 8 * LANES), jnp.float32))
        piece = jnp.concatenate(chunks, axis=1)
        pieces.append(piece if d == 0 else pltpu.roll(piece, d * points, 1))
    erow[...] = pieces[0] + pieces[1] + pieces[2]
    modal = lax.dot_general(
        erow[:, : 3 * points].astype(jnp.bfloat16),
        shapes[...],
        NN,
        preferred_element_type=jnp.float32,
    )[0:1]
    vel_new = vel_in[...] + modal_step * (modal - stiff_in[...])
    vel_out[...] = vel_new
    disp_out[...] = disp_in[...] + modal_step * vel_new

    z_copy.wait_recv()
    column = z_in[...]
    for k in range(9):
        up, down = 3 * k + 2, 3 * k
        above = column if k == 0 else pltpu.roll(column, LANES - k, 1)
        cells[up] = jnp.where(
            lane == 0, jnp.where(at_bottom, inflow[up], above), pltpu.roll(cells[up], 1, 1)
        )
        cells[down] = jnp.where(
            lane == LANES - 1,
            jnp.where(at_bottom, pltpu.roll(column, LANES - 1 - k, 1), inflow[down]),
            pltpu.roll(cells[down], LANES - 1, 1),
        )

    ups = [i for i in range(27) if i // 3 % 3 == 2]
    downs = [i for i in range(27) if i // 3 % 3 == 0]
    for k in range(9):
        for x in range(size_x):
            spot = k * size_x + x
            last = (x + 1) * size_y - 1
            y_send[0, spot : spot + 1, :] = cells[ups[k], last : last + 1, :]
            first = x * size_y
            y_send[1, spot : spot + 1, :] = cells[downs[k], first : first + 1, :]
    y_copies = [
        send(y_send.at[0], y_in.at[0], (gx, lax.rem(gy + 1, columns), gz)),
        send(y_send.at[1], y_in.at[1], (gx, lax.rem(gy + columns - 1, columns), gz)),
    ]
    row = lax.broadcasted_iota(jnp.int32, (size_y, LANES), 0)
    for copy in y_copies:
        copy.wait_recv()
    for k in range(9):
        for x in range(size_x):
            spot = k * size_x + x
            span = slice(x * size_y, (x + 1) * size_y)
            up, down = ups[k], downs[k]
            below = jnp.where(gy == 0, inflow[up], y_in[0, spot : spot + 1, :])
            cells[up, span, :] = jnp.where(row == 0, below, pltpu.roll(cells[up, span, :], 1, 0))
            above = jnp.where(gy == columns - 1, inflow[down], y_in[1, spot : spot + 1, :])
            cells[down, span, :] = jnp.where(
                row == size_y - 1, above, pltpu.roll(cells[down, span, :], size_y - 1, 0)
            )

    tail = plane - size_y
    x_copies = [
        send(cells.at[pl.ds(18, 9), pl.ds(tail, size_y)], x_in.at[0], far_id(1)),
        send(cells.at[pl.ds(0, 9), pl.ds(0, size_y)], x_in.at[1], far_id(slabs - 1)),
    ]
    pops_out[9:18] = cells[9:18]
    pops_out[18:27, size_y:, :] = cells[18:27, :tail, :]
    pops_out[0:9, :tail, :] = cells[0:9, size_y:, :]
    for copy in x_copies:
        copy.wait_recv()
    pops_out[18:27, :size_y, :] = x_in[0]
    pops_out[0:9, tail:, :] = x_in[1]
    for copy in started:
        copy.wait_send()


def body(
    sizes,
    populations,
    relax,
    entry_point,
    entry_offset,
    entry_weight,
    entry_count,
    turbine_owner,
    mode_shapes,
    coupling,
    modal_disp,
    modal_vel,
    rigid_vel,
    drag_coef,
):
    slabs, columns, layers = sizes
    _, size_x, size_y, size_z = populations.shape
    points = drag_coef.shape[1]
    modes = modal_vel.shape[1]
    capacity = entry_point.shape[0]
    plane = size_x * size_y
    padded = -(-slabs // 8) * 8
    rows = 3 * padded
    ranks = columns * layers
    width = -(-3 * points // LANES) * LANES
    assert ranks == 8 and layers == 2 and size_z == LANES and points <= 8 * LANES
    stiff = jnp.dot(coupling[0], modal_disp[0], precision=highest)[None, :]
    aux = jnp.concatenate([rigid_vel[0], drag_coef], axis=0)
    aux = jnp.pad(aux, ((0, 4), (0, 8 * LANES - points)))
    aux = aux.reshape(8, 8, LANES).transpose(1, 0, 2)
    copies = 2 * (slabs - 1) + 2 * (ranks - 1) + 5
    vmem = pl.BlockSpec(memory_space=pltpu.VMEM)
    smem = pl.BlockSpec(memory_space=pltpu.SMEM)
    full = jnp.float32
    half = jnp.bfloat16
    out = pl.pallas_call(
        functools.partial(kernel, (slabs, columns, layers, points, size_x, size_y)),
        out_shape=(
            jax.ShapeDtypeStruct((27, plane, size_z), full),
            jax.ShapeDtypeStruct((3 * plane, size_z), full),
            jax.ShapeDtypeStruct((1, modes), full),
            jax.ShapeDtypeStruct((1, modes), full),
        ),
        in_specs=[vmem, smem, vmem, vmem, vmem, smem, smem, pl.BlockSpec(memory_space=pl.ANY)]
        + [vmem] * 4,
        out_specs=(vmem,) * 4,
        scratch_shapes=[
            pltpu.VMEM((3 * points, modes), half),
            pltpu.VMEM((27, plane, size_z), full),
            pltpu.VMEM((27, plane, size_z), full),
            pltpu.VMEM((3 * plane, 2 * LANES), half),
            pltpu.VMEM((TILE_SIDE, LANES, capacity), half),
            pltpu.VMEM((TILE_SIDE, plane, capacity), full),
            pltpu.VMEM((LANES, capacity), half),
            pltpu.VMEM((8, rows, LANES), full),
            pltpu.VMEM((ranks - 1, rows, LANES), full),
            pltpu.VMEM((rows, LANES), full),
            pltpu.VMEM((slabs - 1, rows, LANES), full),
            pltpu.VMEM((8, 8, LANES), full),
            pltpu.VMEM((slabs, 8, LANES), full),
            pltpu.VMEM((rows, LANES), full),
            pltpu.VMEM((8, rows, LANES), full),
            pltpu.VMEM((8, width), full),
            pltpu.VMEM((3 * plane, LANES), full),
            pltpu.VMEM((plane, LANES), full),
            pltpu.VMEM((plane, LANES), full),
            pltpu.VMEM((2, 9 * size_x + 4, LANES), full),
            pltpu.VMEM((2, 9 * size_x + 4, LANES), full),
            pltpu.VMEM((2, 9, size_y, LANES), full),
            pltpu.SemaphoreType.DMA,
            pltpu.SemaphoreType.DMA((copies,)),
            pltpu.SemaphoreType.DMA((copies,)),
        ],
        compiler_params=pltpu.CompilerParams(
            collective_id=0, has_side_effects=True, vmem_limit_bytes=40 * 1024 * 1024
        ),
    )(
        populations.reshape(27, plane, size_z),
        relax,
        entry_point[None, :],
        entry_offset,
        entry_weight,
        entry_count,
        turbine_owner,
        mode_shapes[0],
        stiff,
        modal_disp,
        modal_vel,
        aux,
    )
    populations_out, body_force, disp_new, vel_new = out
    return (
        populations_out.reshape(populations.shape),
        body_force.reshape(3, size_x, size_y, size_z),
        disp_new,
        vel_new,
    )


def solution(mesh):
    sizes = (mesh.shape["gx"], mesh.shape["gy"], mesh.shape["gz"])
    return jax.shard_map(
        functools.partial(body, sizes),
        mesh=mesh,
        in_specs=(
            P(None, "gx", "gy", "gz"),
            P(),
            P(("gx", "gy", "gz")),
            P(None, ("gx", "gy", "gz")),
            P(None, ("gx", "gy", "gz")),
            P(("gx", "gy", "gz")),
            P(),
            P("gx", None, None),
            P("gx", None, None),
            P("gx", None),
            P("gx", None),
            P("gx", None, None),
            P("gx", None),
        ),
        out_specs=(
            P(None, "gx", "gy", "gz"),
            P(None, "gx", "gy", "gz"),
            P("gx", None),
            P("gx", None),
        ),
        check_vma=False,
    )
```

time: 173 us -> 48.2 us (0.28)
  blocking collectives: 56.7 us -> 0 us
  matrix products: 48.1 us -> 1.66 us
  local copies, waits for them, and re-layouts: 48.5 us -> 11.9 us
  Pallas kernels: 0 us -> 32.1 us
  starting transfers between devices: 7.43 us -> 0 us
  other arithmetic: 6.19 us -> 0.7 us
  waiting for transfers between devices: 3.93 us -> 0 us
    dot_general x16 -> x1, matrix products: 48.1 us -> 1.66 us  [body(): stiff = jnp.dot(coupling[0], modal_disp[0], precision=highest)[None, :]]
    pallas_call x0 -> x1, Pallas kernels: none -> 32.1 us  [body(): pl.pallas_call(functools.partial(kernel, (slabs, columns, layers, points,...]
    psum x1 -> x0, blocking collectives: 22.3 us -> none  [body(): sample = lax.psum(own_sums, ('gy', 'gz'))[:, 0, :]]
    unnamed x1 -> x0, blocking collectives: 21.2 us -> none
    transpose x2 -> x0, local copies, waits for them, and re-layouts: 14.7 us -> none  [body(): jnp.einsum('xbcr,byr->xycr', kernel_xk, select_y, precision=highest)]
    all_gather x1 -> x0, blocking collectives: 13.1 us -> none  [body(): lax.all_gather(blade_force[:, None, :], 'gx', axis=1, tiled=True)]
    slice x8 -> x0, local copies, waits for them, and re-layouts: 9.54 us -> none  [the longest x3 4.79 us: padded_2(): lax.slice_in_dim(cells, cells.shape[dim] - width, cells.shape[dim], axis=...]
    ppermute x6 -> x0, starting transfers between devices: 7.43 us -> none  [the longest x3 5.58 us: padded_2(): lax.ppermute(head, axis, [((i + 1) % count, i) for i in range(count)])]
  transfers between devices with their start and end apart: 6 -> 0, of which waited for: 3 -> 0; matrix products, arithmetic and copies ran while one was open for 6% -> 0% of each run, Pallas kernels for 0% -> 0%
where the time goes in v1:
time: 48.2 us; the launch traced here: 47.7 us
  Pallas kernels  32.1 us (67%)
  local copies, waits for them, and re-layouts  11.9 us (25%)
  matrix products  1.66 us (3%)
  between operations  1.4 us (3%)
  other arithmetic  0.7 us (1%)
    pallas_call x1, Pallas kernels, body(): pl.pallas_call(functools.partial(kernel, (slabs, columns, layers, points,...  32.1 us
    unnamed x25, local copies, waits for them, and re-layouts  11.9 us
    dot_general x1, matrix products, body(): stiff = jnp.dot(coupling[0], modal_disp[0], precision=highest)[None, :]  1.66 us

profile of v1, /device:TPU:0, one launch (start us, length us, event | category | flops | bytes accessed | tf_op | source)
XLA Modules:
  0.0 47.7 jit_solution(7761707069874663253)
XLA Ops:
  0.6 0.0 copy-start
  1.4 0.5 %copy-done = f32[1,512,512]{2,1,0:T(8,128)S(1)} copy-done((f32[1,512,512]{2,1,0:T(8,128)S(1)}, f32[1,512,512]{2,1,0:T(8,128)}, u32[]{:S(2)}) %copy-start) | copy-done | bytes 1048600
  1.9 1.7 %fusion.stiff_in = f32[1,512]{1,0:T(1,128)S(1)} fusion(f32[1,512,512]{2,1,0:T(8,128)S(1)} %copy-done, f32[1,512]{1,0:T(1,128)} %disp_in.1), kind=kOutput, calls=%fused_computation | convolution fusion | flops 3145728 | bytes 1052672 | tf_op jit(solution)/shard_map/dot_general | solution.py:525
  3.5 0.7 %copy.19 = f32[1,3,900]{2,1,0:T(4,128)S(1)} copy(f32[1,3,900]{2,0,1:T(1,128)} %param.24) | data formatting | bytes 21600
  4.3 0.7 %fusion.2.aux_in = f32[8,8,128]{2,1,0:T(8,128)S(1)} fusion(f32[1,900]{1,0:T(1,128)} %param.25, f32[3,900]{1,0:T(4,128)S(1)} %bitcast.25), kind=kLoop, calls=%fused_computation.3 | loop fusion | flops 65536 | bytes 47168 | tf_op jit(solution)/shard_map/transpose | solution.py:528
  5.0 0.0 copy-start.1
  5.0 1.8 %copy-done.1 = bf16[1,2700,512]{2,1,0:T(8,128)(2,1)S(1)} copy-done((bf16[1,2700,512]{2,1,0:T(8,128)(2,1)S(1)}, bf16[1,2700,512]{2,1,0:T(8,128)(2,1)}, u32[]{:S(2)}) %copy-start.1) | copy-done | bytes 2764824
  6.8 0.0 copy-start.2
  6.8 1.2 %copy-done.2 = f32[27,4,16,128]{3,2,1,0:T(8,128)S(1)} copy-done((f32[27,4,16,128]{3,2,1,0:T(8,128)S(1)}, f32[27,4,16,128]{3,2,1,0:T(8,128)}, u32[]{:S(2)}) %copy-start.2) | copy-done | bytes 884760
  7.9 0.0 copy-start.3
  7.9 0.9 %copy-done.3 = f32[64,1024]{1,0:T(8,128)S(1)} copy-done((f32[64,1024]{1,0:T(8,128)S(1)}, f32[64,1024]{1,0:T(8,128)}, u32[]{:S(2)}) %copy-start.3) | copy-done | bytes 262168
  8.9 0.0 copy-start.4
  8.9 0.7 %copy-done.4 = s32[3,1024]{1,0:T(4,128)S(1)} copy-done((s32[3,1024]{1,0:T(4,128)S(1)}, s32[3,1024]{1,0:T(4,128)}, u32[]{:S(2)}) %copy-start.4) | copy-done | bytes 12312
  9.6 0.0 copy-start.5
  9.6 0.7 %copy-done.5 = f32[1,512]{1,0:T(1,128)S(1)} copy-done((f32[1,512]{1,0:T(1,128)S(1)}, f32[1,512]{1,0:T(1,128)}, u32[]{:S(2)}) %copy-start.5) | copy-done | bytes 2072
  10.3 0.0 copy-start.6
  10.3 0.7 %copy-done.6 = s32[1024]{0:T(1024)S(1)} copy-done((s32[1024]{0:T(1024)S(1)}, s32[1024]{0:T(1024)}, u32[]{:S(2)}) %copy-start.6) | copy-done | bytes 4120
  11.0 0.0 copy-start.7
  11.0 0.7 %copy-done.7 = f32[1,512]{1,0:T(1,128)S(1)} copy-done((f32[1,512]{1,0:T(1,128)S(1)}, f32[1,512]{1,0:T(1,128)}, u32[]{:S(2)}) %copy-start.7) | copy-done | bytes 2072
  11.6 0.0 copy-start.8
  11.6 0.7 %copy-done.8 = f32[27]{0:T(128)S(1)} copy-done((f32[27]{0:T(128)S(1)}, f32[27]{0:T(128)}, u32[]{:S(2)}) %copy-start.8) | copy-done | bytes 132
  12.3 0.0 copy-start.9
  12.3 0.7 %copy-done.9 = s32[4]{0:T(128)S(1)} copy-done((s32[4]{0:T(128)S(1)}, s32[4]{0:T(128)}, u32[]{:S(2)}) %copy-start.9) | copy-done | bytes 40
  13.0 32.1 %shard_map.156 = (f32[27,64,128]{2,1,0:T(8,128)S(1)}, f32[192,128]{1,0:T(8,128)S(1)}, f32[1,512]{1,0:T(1,128)S(1)}, f32[1,512]{1,0:T(1,128)S(1)}) custom-call(f32[27,64,128]{2,1,0:T(8,128)S(1)} %bitcast.21, f32[27]{0:T(128)S(1)} %copy-done.8, s32[1,1024]{1,0:T(1,128)S(1)} %bitcast.24, s32[3,1024]{1,0:T(4,128)S(1)} %copy-done.4, f32[64,1024]{1,0:T(8,128)S(1)} %copy-done.3, ...), custom_call_target="tpu_custom_call" | custom-call | tf_op jit(solution)/shard_map/pallas_call | solution.py:534
  45.0 0.9 %copy.25 = f32[27,4,16,128]{3,2,1,0:T(8,128)} copy(f32[27,4,16,128]{3,2,1,0:T(8,128)S(1)} %bitcast.22) | data formatting | bytes 1769472
  45.9 0.6 %copy.26 = f32[3,4,16,128]{3,2,1,0:T(8,128)} copy(f32[3,4,16,128]{3,2,1,0:T(8,128)S(1)} %bitcast.23) | data formatting | bytes 196608
  46.6 0.6 %copy.27 = f32[1,512]{1,0:T(1,128)} copy(f32[1,512]{1,0:T(1,128)S(1)} %get-tuple-element.18) | data formatting | bytes 4096
  47.2 0.6 %copy.28 = f32[1,512]{1,0:T(1,128)} copy(f32[1,512]{1,0:T(1,128)S(1)} %get-tuple-element.19) | data formatting | bytes 4096
Async XLA Ops:
  0.6 1.2 %copy-start = (f32[1,512,512]{2,1,0:T(8,128)S(1)}, f32[1,512,512]{2,1,0:T(8,128)}, u32[]{:S(2)}) copy-start(f32[1,512,512]{2,1,0:T(8,128)} %param.21) | copy-start | bytes 3145732
  5.0 1.8 %copy-start.1 = (bf16[1,2700,512]{2,1,0:T(8,128)(2,1)S(1)}, bf16[1,2700,512]{2,1,0:T(8,128)(2,1)}, u32[]{:S(2)}) copy-start(bf16[1,2700,512]{2,1,0:T(8,128)(2,1)} %param.20) | copy-start | bytes 8294404
  6.8 1.2 %copy-start.2 = (f32[27,4,16,128]{3,2,1,0:T(8,128)S(1)}, f32[27,4,16,128]{3,2,1,0:T(8,128)}, u32[]{:S(2)}) copy-start(f32[27,4,16,128]{3,2,1,0:T(8,128)} %param.13) | copy-start | bytes 2654212
  7.9 0.9 %copy-start.3 = (f32[64,1024]{1,0:T(8,128)S(1)}, f32[64,1024]{1,0:T(8,128)}, u32[]{:S(2)}) copy-start(f32[64,1024]{1,0:T(8,128)} %weight_in.1) | copy-start | bytes 786436
  8.9 0.7 %copy-start.4 = (s32[3,1024]{1,0:T(4,128)S(1)}, s32[3,1024]{1,0:T(4,128)}, u32[]{:S(2)}) copy-start(s32[3,1024]{1,0:T(4,128)} %offset_in.1) | copy-start | bytes 36868
  9.6 0.7 %copy-start.5 = (f32[1,512]{1,0:T(1,128)S(1)}, f32[1,512]{1,0:T(1,128)}, u32[]{:S(2)}) copy-start(f32[1,512]{1,0:T(1,128)} %disp_in.1) | copy-start | bytes 6148
  10.3 0.7 %copy-start.6 = (s32[1024]{0:T(1024)S(1)}, s32[1024]{0:T(1024)}, u32[]{:S(2)}) copy-start(s32[1024]{0:T(1024)} %param.15) | copy-start | bytes 12292
  11.0 0.7 %copy-start.7 = (f32[1,512]{1,0:T(1,128)S(1)}, f32[1,512]{1,0:T(1,128)}, u32[]{:S(2)}) copy-start(f32[1,512]{1,0:T(1,128)} %vel_in.1) | copy-start | bytes 6148
  11.6 0.7 %copy-start.8 = (f32[27]{0:T(128)S(1)}, f32[27]{0:T(128)}, u32[]{:S(2)}) copy-start(f32[27]{0:T(128)} %relax.1) | copy-start | bytes 328
  12.3 0.7 %copy-start.9 = (s32[4]{0:T(128)S(1)}, s32[4]{0:T(128)}, u32[]{:S(2)}) copy-start(s32[4]{0:T(128)} %owner_in.1) | copy-start | bytes 52

commit v2 on v1

--- a/solution.py
+++ b/solution.py
@@ -11,6 +11,7 @@
 TILE_SIDE = 4
 LANES = 128
 CHUNK = 256
+VMEM_BYTES = 64 * 1024 * 1024
 MESH = pl.DeviceIdType.MESH
 
 highest = lax.Precision.HIGHEST
@@ -66,6 +67,23 @@
 
 def kernel(
     sizes,
+    pops_hbm,
+    relax_hbm,
+    point_hbm,
+    offset_hbm,
+    weight_hbm,
+    count_hbm,
+    owner_hbm,
+    shapes_hbm,
+    coupling_hbm,
+    disp_hbm,
+    vel_hbm,
+    rigid_hbm,
+    drag_hbm,
+    pops_out,
+    force_out,
+    disp_out,
+    vel_out,
     pops,
     relax,
     point_in,
@@ -73,16 +91,13 @@
     weight_in,
     count_in,
     owner_in,
-    shapes_hbm,
-    stiff_in,
+    shapes,
+    coupling,
     disp_in,
     vel_in,
+    rigid_in,
+    drag_in,
     aux_in,
-    pops_out,
-    force_out,
-    disp_out,
-    vel_out,
-    shapes,
     moments,
     cells,
     raw_pair,
@@ -120,8 +135,26 @@
     rank = gy * layers + gz
     inflow = inflow_values()
 
-    load_shapes = pltpu.make_async_copy(shapes_hbm, shapes, copy_sem)
-    load_shapes.start()
+    loads = {}
+    for number, (name, src, dst) in enumerate(
+        (
+            ("pops", pops_hbm, pops),
+            ("vel", vel_hbm, vel_in),
+            ("rigid", rigid_hbm, rigid_in),
+            ("drag", drag_hbm, drag_in),
+            ("shapes", shapes_hbm, shapes),
+            ("count", count_hbm, count_in),
+            ("owner", owner_hbm, owner_in),
+            ("point", point_hbm, point_in),
+            ("offset", offset_hbm, offset_in),
+            ("weight", weight_hbm, weight_in),
+            ("relax", relax_hbm, relax),
+            ("disp", disp_hbm, disp_in),
+            ("coupling", coupling_hbm, coupling),
+        )
+    ):
+        loads[name] = pltpu.make_async_copy(src, dst, copy_sem.at[number])
+        loads[name].start()
 
     def slab_peer(step):
         return lax.rem(rank + step, ranks)
@@ -156,6 +189,8 @@
         copy.start()
         started.append(copy)
         return copy
+
+    loads["pops"].wait()
 
     def moments_of(step, _):
         part = pl.ds(pl.multiple_of(step * 8, 8), 8)
@@ -174,7 +209,12 @@
     raw_pair[:, :LANES] = raw_high
     raw_pair[:, LANES:] = raw_low
 
-    load_shapes.wait()
+    for name in ("vel", "rigid", "drag", "shapes"):
+        loads[name].wait()
+    aux_in[...] = jnp.zeros_like(aux_in)
+    for d in range(3):
+        aux_in[d : d + 1, :points] = rigid_in[d]
+    aux_in[3:4, :points] = drag_in[...]
     vel8 = jnp.broadcast_to(vel_in[...], (8, vel_in.shape[1])).astype(jnp.bfloat16)
     erow[...] = jnp.zeros_like(erow)
     erow[:, : 3 * points] = lax.dot_general(
@@ -195,13 +235,15 @@
             jnp.where(row8 == 1, shifted[1][:, spot], shifted[2][:, spot]),
         )
         inside = (row8 < 3) & (lane8 + jh * LANES < points)
-        aux[jh] = aux_in[jh] + jnp.where(inside, both, 0.0)
+        aux[jh] = aux_in[:, spot] + jnp.where(inside, both, 0.0)
     pl.semaphore_wait(barrier, slabs - 1 + ranks - 1)
     aux_copies = [
         send(aux.at[rank], aux_all.at[gx], far_id(step)) for step in range(1, slabs)
     ]
     aux_all[gx] = aux[rank]
 
+    for name in ("count", "owner", "point", "offset", "weight"):
+        loads[name].wait()
     dense[...] = jnp.zeros_like(dense)
     count = count_in[0]
     iota_y = lax.broadcasted_iota(jnp.int32, (size_y, CHUNK), 0)
@@ -346,6 +388,8 @@
 
     lax.fori_loop(0, capacity // CHUNK, scatter, 0)
     force_out[...] = -spread[...]
+
+    loads["relax"].wait()
 
     def collide(step, _):
         part = pl.ds(pl.multiple_of(step * 8, 8), 8)
@@ -433,7 +477,13 @@
         NN,
         preferred_element_type=jnp.float32,
     )[0:1]
-    vel_new = vel_in[...] + modal_step * (modal - stiff_in[...])
+    loads["disp"].wait()
+    loads["coupling"].wait()
+    disp8 = jnp.broadcast_to(disp_in[...], (8, disp_in.shape[1]))
+    stiff = lax.dot_general(
+        disp8, coupling[...], NT, precision=highest, preferred_element_type=jnp.float32
+    )[0:1]
+    vel_new = vel_in[...] + modal_step * (modal - stiff)
     vel_out[...] = vel_new
     disp_out[...] = disp_in[...] + modal_step * vel_new
 
@@ -495,6 +545,19 @@
         copy.wait_send()
 
 
+def store_kernel(a, b, c, d, a_out, b_out, c_out, d_out, sems):
+    pairs = [(a.at[pl.ds(i, 9)], a_out.at[pl.ds(i, 9)]) for i in (0, 9, 18)]
+    pairs += [(b, b_out), (c, c_out), (d, d_out)]
+    copies = [
+        pltpu.make_async_copy(src, dst, sems.at[number])
+        for number, (src, dst) in enumerate(pairs)
+    ]
+    for copy in copies:
+        copy.start()
+    for copy in copies:
+        copy.wait()
+
+
 def body(
     sizes,
     populations,
@@ -522,13 +585,10 @@
     ranks = columns * layers
     width = -(-3 * points // LANES) * LANES
     assert ranks == 8 and layers == 2 and size_z == LANES and points <= 8 * LANES
-    stiff = jnp.dot(coupling[0], modal_disp[0], precision=highest)[None, :]
-    aux = jnp.concatenate([rigid_vel[0], drag_coef], axis=0)
-    aux = jnp.pad(aux, ((0, 4), (0, 8 * LANES - points)))
-    aux = aux.reshape(8, 8, LANES).transpose(1, 0, 2)
     copies = 2 * (slabs - 1) + 2 * (ranks - 1) + 5
     vmem = pl.BlockSpec(memory_space=pltpu.VMEM)
-    smem = pl.BlockSpec(memory_space=pltpu.SMEM)
+    hbm = pl.BlockSpec(memory_space=pltpu.HBM)
+    whole = jnp.int32
     full = jnp.float32
     half = jnp.bfloat16
     out = pl.pallas_call(
@@ -539,11 +599,23 @@
             jax.ShapeDtypeStruct((1, modes), full),
             jax.ShapeDtypeStruct((1, modes), full),
         ),
-        in_specs=[vmem, smem, vmem, vmem, vmem, smem, smem, pl.BlockSpec(memory_space=pl.ANY)]
-        + [vmem] * 4,
+        in_specs=[hbm] * 13,
         out_specs=(vmem,) * 4,
         scratch_shapes=[
+            pltpu.VMEM((27, plane, size_z), full),
+            pltpu.SMEM(relax.shape, full),
+            pltpu.VMEM((1, capacity), whole),
+            pltpu.VMEM(entry_offset.shape, whole),
+            pltpu.VMEM(entry_weight.shape, full),
+            pltpu.SMEM(entry_count.shape, whole),
+            pltpu.SMEM(turbine_owner.shape, whole),
             pltpu.VMEM((3 * points, modes), half),
+            pltpu.VMEM((modes, modes), full),
+            pltpu.VMEM((1, modes), full),
+            pltpu.VMEM((1, modes), full),
+            pltpu.VMEM((3, 1, points), full),
+            pltpu.VMEM((1, points), full),
+            pltpu.VMEM((8, 8 * LANES), full),
             pltpu.VMEM((27, plane, size_z), full),
             pltpu.VMEM((27, plane, size_z), full),
             pltpu.VMEM((3 * plane, 2 * LANES), half),
@@ -565,12 +637,12 @@
             pltpu.VMEM((2, 9 * size_x + 4, LANES), full),
             pltpu.VMEM((2, 9 * size_x + 4, LANES), full),
             pltpu.VMEM((2, 9, size_y, LANES), full),
-            pltpu.SemaphoreType.DMA,
+            pltpu.SemaphoreType.DMA((13,)),
             pltpu.SemaphoreType.DMA((copies,)),
             pltpu.SemaphoreType.DMA((copies,)),
         ],
         compiler_params=pltpu.CompilerParams(
-            collective_id=0, has_side_effects=True, vmem_limit_bytes=40 * 1024 * 1024
+            collective_id=0, has_side_effects=True, vmem_limit_bytes=VMEM_BYTES
         ),
     )(
         populations.reshape(27, plane, size_z),
@@ -581,12 +653,22 @@
         entry_count,
         turbine_owner,
         mode_shapes[0],
-        stiff,
+        coupling[0],
         modal_disp,
         modal_vel,
-        aux,
+        rigid_vel.transpose(1, 0, 2),
+        drag_coef,
     )
-    populations_out, body_force, disp_new, vel_new = out
+    populations_out, body_force, disp_new, vel_new = pl.pallas_call(
+        store_kernel,
+        out_shape=tuple(jax.ShapeDtypeStruct(o.shape, o.dtype) for o in out),
+        in_specs=[hbm] * 4,
+        out_specs=(hbm,) * 4,
+        scratch_shapes=[pltpu.SemaphoreType.DMA((6,))],
+        compiler_params=pltpu.CompilerParams(
+            has_side_effects=True, vmem_limit_bytes=VMEM_BYTES
+        ),
+    )(*out)
     return (
         populations_out.reshape(populations.shape),
         body_force.reshape(3, size_x, size_y, size_z),

time: 48.2 us -> 65.5 us (1.36)
  Pallas kernels: 32.1 us -> 64.1 us
  local copies, waits for them, and re-layouts: 11.9 us -> 0 us
  matrix products: 1.66 us -> 0 us
  other arithmetic: 0.7 us -> 0 us
    pallas_call x0 -> x1, Pallas kernels: none -> 31.1 us  [body(): pl.pallas_call(store_kernel, out_shape=tuple((jax.ShapeDtypeStruct(o.shap...]
    unnamed x25 -> x0, local copies, waits for them, and re-layouts: 11.9 us -> none
    dot_general x1 -> x0, matrix products: 1.66 us -> none  [body(): stiff = jnp.dot(coupling[0], modal_disp[0], precision=highest)[None, :]]
    pallas_call x1, Pallas kernels: 32.1 us -> 33 us  [body(): pl.pallas_call(functools.partial(kernel, (slabs, columns, layers, points,...]
    transpose x1 -> x0, other arithmetic: 0.7 us -> none  [body(): aux = aux.reshape(8, 8, LANES).transpose(1, 0, 2)]
where the time goes in v2:
time: 65.5 us; the launch traced here: 65.4 us
  Pallas kernels  64.1 us (98%)
  between operations  1.29 us (2%)
    pallas_call x1, Pallas kernels, body(): pl.pallas_call(functools.partial(kernel, (slabs, columns, layers, points,...  33 us
    pallas_call x1, Pallas kernels, body(): pl.pallas_call(store_kernel, out_shape=tuple((jax.ShapeDtypeStruct(o.shap...  31.1 us

profile of v2, /device:TPU:0, one launch (start us, length us, event | category | flops | bytes accessed | tf_op | source)
XLA Modules:
  0.0 65.4 jit_solution(11153075183957924333)
XLA Ops:
  1.3 33.0 %shard_map.156 = (f32[27,64,128]{2,1,0:T(8,128)}, f32[192,128]{1,0:T(8,128)}, f32[1,512]{1,0:T(1,128)}, f32[1,512]{1,0:T(1,128)}) custom-call(f32[27,64,128]{2,1,0:T(8,128)} %bitcast.9, f32[27]{0:T(128)} %relax_hbm.1, s32[1,1024]{1,0:T(1,128)} %bitcast.11, s32[3,1024]{1,0:T(4,128)} %offset_hbm.1, f32[64,1024]{1,0:T(8,128)} %weight_hbm.1, ...), custom_call_target="tpu_custom_call" | custom-call | tf_op jit(solution)/shard_map/pallas_call | solution.py:594
  34.3 31.1 %shard_map.157 = (f32[27,64,128]{2,1,0:T(8,128)}, f32[192,128]{1,0:T(8,128)}, f32[1,512]{1,0:T(1,128)}, f32[1,512]{1,0:T(1,128)}) custom-call(f32[27,64,128]{2,1,0:T(8,128)} %get-tuple-element.12.a, f32[192,128]{1,0:T(8,128)} %get-tuple-element.13.b, f32[1,512]{1,0:T(1,128)} %get-tuple-element.14.c, f32[1,512]{1,0:T(1,128)} %get-tuple-element.15.d), custom_call_target="tpu_custom_call" | custom-call | tf_op jit(solution)/shard_map/pallas_call | solution.py:662

commit v3 on v2

--- a/solution.py
+++ b/solution.py
@@ -80,7 +80,10 @@
     vel_hbm,
     rigid_hbm,
     drag_hbm,
-    pops_out,
+    pops_hbm_out,
+    force_hbm_out,
+    disp_hbm_out,
+    vel_hbm_out,
     force_out,
     disp_out,
     vel_out,
@@ -120,6 +123,7 @@
     y_in,
     x_in,
     copy_sem,
+    store_sem,
     send_sem,
     recv_sem,
 ):
@@ -172,6 +176,13 @@
         pl.semaphore_signal(
             barrier, inc=1, device_id=slab_id(slab_peer(step)), device_id_type=MESH
         )
+
+    stores = []
+
+    def store(src, dst):
+        copy = pltpu.make_async_copy(src, dst, store_sem.at[len(stores)])
+        copy.start()
+        stores.append(copy)
 
     used = [0]
     started = []
@@ -388,6 +399,7 @@
 
     lax.fori_loop(0, capacity // CHUNK, scatter, 0)
     force_out[...] = -spread[...]
+    store(force_out, force_hbm_out)
 
     loads["relax"].wait()
 
@@ -486,6 +498,8 @@
     vel_new = vel_in[...] + modal_step * (modal - stiff)
     vel_out[...] = vel_new
     disp_out[...] = disp_in[...] + modal_step * vel_new
+    store(vel_out, vel_hbm_out)
+    store(disp_out, disp_hbm_out)
 
     z_copy.wait_recv()
     column = z_in[...]
@@ -534,28 +548,37 @@
         send(cells.at[pl.ds(18, 9), pl.ds(tail, size_y)], x_in.at[0], far_id(1)),
         send(cells.at[pl.ds(0, 9), pl.ds(0, size_y)], x_in.at[1], far_id(slabs - 1)),
     ]
-    pops_out[9:18] = cells[9:18]
-    pops_out[18:27, size_y:, :] = cells[18:27, :tail, :]
-    pops_out[0:9, :tail, :] = cells[0:9, size_y:, :]
-    for copy in x_copies:
-        copy.wait_recv()
-    pops_out[18:27, :size_y, :] = x_in[0]
-    pops_out[0:9, tail:, :] = x_in[1]
+    low, mid, high = (pl.ds(i, 9) for i in (0, 9, 18))
+    inner, outer = pl.ds(0, tail), pl.ds(size_y, tail)
+    first, last = pl.ds(0, size_y), pl.ds(tail, size_y)
+    store(cells.at[mid], pops_hbm_out.at[mid])
+    store(cells.at[high, inner], pops_hbm_out.at[high, outer])
+    store(cells.at[low, outer], pops_hbm_out.at[low, inner])
+    x_copies[0].wait_recv()
+    store(x_in.at[0], pops_hbm_out.at[high, first])
+    x_copies[1].wait_recv()
+    store(x_in.at[1], pops_hbm_out.at[low, last])
+    for copy in stores:
+        copy.wait()
     for copy in started:
         copy.wait_send()
 
 
-def store_kernel(a, b, c, d, a_out, b_out, c_out, d_out, sems):
-    pairs = [(a.at[pl.ds(i, 9)], a_out.at[pl.ds(i, 9)]) for i in (0, 9, 18)]
-    pairs += [(b, b_out), (c, c_out), (d, d_out)]
-    copies = [
-        pltpu.make_async_copy(src, dst, sems.at[number])
-        for number, (src, dst) in enumerate(pairs)
-    ]
-    for copy in copies:
-        copy.start()
-    for copy in copies:
-        copy.wait()
+def store_kernel(*refs):
+    sources, targets, held = refs[0:4], refs[4:8], refs[8:12]
+    load_sem, store_sem = refs[12:]
+    parts = [(0, pl.ds(i, 9)) for i in (9, 18, 0)] + [(k, slice(None)) for k in (1, 2, 3)]
+    loads, stores = [], []
+    for number, (k, part) in enumerate(parts):
+        here = held[k].at[part]
+        loads.append(pltpu.make_async_copy(sources[k].at[part], here, load_sem.at[number]))
+        stores.append(pltpu.make_async_copy(here, targets[k].at[part], store_sem.at[number]))
+        loads[-1].start()
+    for load, store in zip(loads, stores):
+        load.wait()
+        store.start()
+    for store in stores:
+        store.wait()
 
 
 def body(
@@ -586,7 +609,6 @@
     width = -(-3 * points // LANES) * LANES
     assert ranks == 8 and layers == 2 and size_z == LANES and points <= 8 * LANES
     copies = 2 * (slabs - 1) + 2 * (ranks - 1) + 5
-    vmem = pl.BlockSpec(memory_space=pltpu.VMEM)
     hbm = pl.BlockSpec(memory_space=pltpu.HBM)
     whole = jnp.int32
     full = jnp.float32
@@ -600,8 +622,11 @@
             jax.ShapeDtypeStruct((1, modes), full),
         ),
         in_specs=[hbm] * 13,
-        out_specs=(vmem,) * 4,
+        out_specs=(hbm,) * 4,
         scratch_shapes=[
+            pltpu.VMEM((3 * plane, size_z), full),
+            pltpu.VMEM((1, modes), full),
+            pltpu.VMEM((1, modes), full),
             pltpu.VMEM((27, plane, size_z), full),
             pltpu.SMEM(relax.shape, full),
             pltpu.VMEM((1, capacity), whole),
@@ -638,6 +663,7 @@
             pltpu.VMEM((2, 9 * size_x + 4, LANES), full),
             pltpu.VMEM((2, 9, size_y, LANES), full),
             pltpu.SemaphoreType.DMA((13,)),
+            pltpu.SemaphoreType.DMA((8,)),
             pltpu.SemaphoreType.DMA((copies,)),
             pltpu.SemaphoreType.DMA((copies,)),
         ],
@@ -664,7 +690,8 @@
         out_shape=tuple(jax.ShapeDtypeStruct(o.shape, o.dtype) for o in out),
         in_specs=[hbm] * 4,
         out_specs=(hbm,) * 4,
-        scratch_shapes=[pltpu.SemaphoreType.DMA((6,))],
+        scratch_shapes=[pltpu.VMEM(o.shape, o.dtype) for o in out]
+        + [pltpu.SemaphoreType.DMA((6,))] * 2,
         compiler_params=pltpu.CompilerParams(
             has_side_effects=True, vmem_limit_bytes=VMEM_BYTES
         ),

time: 65.5 us -> 36.2 us (0.55)
  Pallas kernels: 64.1 us -> 34.8 us
    pallas_call x1, Pallas kernels: 31.1 us -> 2 us  [body(): pl.pallas_call(store_kernel, out_shape=tuple((jax.ShapeDtypeStruct(o.shap...]
where the time goes in v3:
time: 36.2 us; the launch traced here: 36.1 us
  Pallas kernels  34.8 us (96%)
  between operations  1.29 us (4%)
    pallas_call x1, Pallas kernels, body(): pl.pallas_call(functools.partial(kernel, (slabs, columns, layers, points,...  32.8 us
    pallas_call x1, Pallas kernels, body(): pl.pallas_call(store_kernel, out_shape=tuple((jax.ShapeDtypeStruct(o.shap...  2 us

profile of v3, /device:TPU:0, one launch (start us, length us, event | category | flops | bytes accessed | tf_op | source)
XLA Modules:
  0.0 36.1 jit_solution(278532902455997498)
XLA Ops:
  1.3 32.8 %shard_map.156 = (f32[27,64,128]{2,1,0:T(8,128)}, f32[192,128]{1,0:T(8,128)}, f32[1,512]{1,0:T(1,128)}, f32[1,512]{1,0:T(1,128)}) custom-call(f32[27,64,128]{2,1,0:T(8,128)} %bitcast.9, f32[27]{0:T(128)} %relax_hbm.1, s32[1,1024]{1,0:T(1,128)} %bitcast.11, s32[3,1024]{1,0:T(4,128)} %offset_hbm.1, f32[64,1024]{1,0:T(8,128)} %weight_hbm.1, ...), custom_call_target="tpu_custom_call" | custom-call | tf_op jit(solution)/shard_map/pallas_call | solution.py:616
  34.1 2.0 %shard_map.157 = (f32[27,64,128]{2,1,0:T(8,128)}, f32[192,128]{1,0:T(8,128)}, f32[1,512]{1,0:T(1,128)}, f32[1,512]{1,0:T(1,128)}) custom-call(f32[27,64,128]{2,1,0:T(8,128)} %get-tuple-element.12.refs_0_, f32[192,128]{1,0:T(8,128)} %get-tuple-element.13.refs_1_, f32[1,512]{1,0:T(1,128)} %get-tuple-element.14.refs_2_, f32[1,512]{1,0:T(1,128)} %get-tuple-element.15.refs_3_), custom_call_target="tpu_custom_call" | custom-call | tf_op jit(solution)/shard_map/pallas_call | solution.py:688

commit v4 on v3

--- a/solution.py
+++ b/solution.py
@@ -121,6 +121,7 @@
     z_in,
     y_send,
     y_in,
+    z_edge,
     x_in,
     copy_sem,
     store_sem,
@@ -143,15 +144,15 @@
     for number, (name, src, dst) in enumerate(
         (
             ("pops", pops_hbm, pops),
-            ("vel", vel_hbm, vel_in),
-            ("rigid", rigid_hbm, rigid_in),
-            ("drag", drag_hbm, drag_in),
-            ("shapes", shapes_hbm, shapes),
             ("count", count_hbm, count_in),
             ("owner", owner_hbm, owner_in),
             ("point", point_hbm, point_in),
             ("offset", offset_hbm, offset_in),
             ("weight", weight_hbm, weight_in),
+            ("vel", vel_hbm, vel_in),
+            ("rigid", rigid_hbm, rigid_in),
+            ("drag", drag_hbm, drag_in),
+            ("shapes", shapes_hbm, shapes),
             ("relax", relax_hbm, relax),
             ("disp", disp_hbm, disp_in),
             ("coupling", coupling_hbm, coupling),
@@ -219,39 +220,6 @@
     raw_high, raw_low = halves(spread[...])
     raw_pair[:, :LANES] = raw_high
     raw_pair[:, LANES:] = raw_low
-
-    for name in ("vel", "rigid", "drag", "shapes"):
-        loads[name].wait()
-    aux_in[...] = jnp.zeros_like(aux_in)
-    for d in range(3):
-        aux_in[d : d + 1, :points] = rigid_in[d]
-    aux_in[3:4, :points] = drag_in[...]
-    vel8 = jnp.broadcast_to(vel_in[...], (8, vel_in.shape[1])).astype(jnp.bfloat16)
-    erow[...] = jnp.zeros_like(erow)
-    erow[:, : 3 * points] = lax.dot_general(
-        vel8, shapes[...], NT, preferred_element_type=jnp.float32
-    )
-    width = erow.shape[1]
-    line = erow[...]
-    shifted = [
-        line if c == 0 else pltpu.roll(line, width - c * points, 1) for c in range(3)
-    ]
-    row8 = lax.broadcasted_iota(jnp.int32, (8, LANES), 0)
-    lane8 = lax.broadcasted_iota(jnp.int32, (8, LANES), 1)
-    for jh in range(8):
-        spot = slice(jh * LANES, (jh + 1) * LANES)
-        both = jnp.where(
-            row8 == 0,
-            shifted[0][:, spot],
-            jnp.where(row8 == 1, shifted[1][:, spot], shifted[2][:, spot]),
-        )
-        inside = (row8 < 3) & (lane8 + jh * LANES < points)
-        aux[jh] = aux_in[:, spot] + jnp.where(inside, both, 0.0)
-    pl.semaphore_wait(barrier, slabs - 1 + ranks - 1)
-    aux_copies = [
-        send(aux.at[rank], aux_all.at[gx], far_id(step)) for step in range(1, slabs)
-    ]
-    aux_all[gx] = aux[rank]
 
     for name in ("count", "owner", "point", "offset", "weight"):
         loads[name].wait()
@@ -324,10 +292,44 @@
 
     lax.fori_loop(0, capacity // CHUNK, gather, 0)
 
+    pl.semaphore_wait(barrier, slabs - 1 + ranks - 1)
+
     first_copies = [
         send(dense.at[slab_peer(step)], dense_in.at[step - 1], slab_id(slab_peer(step)))
         for step in range(1, ranks)
     ]
+    for name in ("vel", "rigid", "drag", "shapes"):
+        loads[name].wait()
+    aux_in[...] = jnp.zeros_like(aux_in)
+    for d in range(3):
+        aux_in[d : d + 1, :points] = rigid_in[d]
+    aux_in[3:4, :points] = drag_in[...]
+    vel8 = jnp.broadcast_to(vel_in[...], (8, vel_in.shape[1])).astype(jnp.bfloat16)
+    erow[...] = jnp.zeros_like(erow)
+    erow[:, : 3 * points] = lax.dot_general(
+        vel8, shapes[...], NT, preferred_element_type=jnp.float32
+    )
+    width = erow.shape[1]
+    line = erow[...]
+    shifted = [
+        line if c == 0 else pltpu.roll(line, width - c * points, 1) for c in range(3)
+    ]
+    row8 = lax.broadcasted_iota(jnp.int32, (8, LANES), 0)
+    lane8 = lax.broadcasted_iota(jnp.int32, (8, LANES), 1)
+    for jh in range(8):
+        spot = slice(jh * LANES, (jh + 1) * LANES)
+        both = jnp.where(
+            row8 == 0,
+            shifted[0][:, spot],
+            jnp.where(row8 == 1, shifted[1][:, spot], shifted[2][:, spot]),
+        )
+        inside = (row8 < 3) & (lane8 + jh * LANES < points)
+        aux[jh] = aux_in[:, spot] + jnp.where(inside, both, 0.0)
+    aux_copies = [
+        send(aux.at[rank], aux_all.at[gx], far_id(step)) for step in range(1, slabs)
+    ]
+    aux_all[gx] = aux[rank]
+
     own = dense[rank]
     for step in range(1, ranks):
         first_copies[step - 1].wait_recv()
@@ -386,13 +388,11 @@
         total = jnp.zeros(spread.shape, jnp.float32)
         for c in range(TILE_SIDE):
             kern = kern_xy[c, :, part]
-            high_part, low_part = halves(
-                jnp.concatenate([kern * forces[d] for d in range(3)], axis=0)
+            weighted = jnp.concatenate(
+                [(kern * forces[d]).astype(jnp.bfloat16) for d in range(3)], axis=0
             )
-            at_z = pick_z[c, :, part]
-            total = total + (
-                lax.dot_general(high_part, at_z, NT, preferred_element_type=jnp.float32)
-                + lax.dot_general(low_part, at_z, NT, preferred_element_type=jnp.float32)
+            total = total + lax.dot_general(
+                weighted, pick_z[c, :, part], NT, preferred_element_type=jnp.float32
             )
         spread[...] += total
         return 0
@@ -471,7 +471,28 @@
         )
         packed = jnp.where(lane == k, column, packed)
     z_send[...] = packed
-    z_copy = send(z_send, z_in, (gx, gy, 1 - gz))
+    next_y = lax.rem(gy + 1, columns)
+    past_y = lax.rem(gy + columns - 1, columns)
+    edge_copies = [
+        send(z_send, z_in.at[0], (gx, gy, 1 - gz)),
+        send(z_send, z_in.at[1], (gx, next_y, 1 - gz)),
+        send(z_send, z_in.at[2], (gx, past_y, 1 - gz)),
+    ]
+    ups = [i for i in range(27) if i // 3 % 3 == 2]
+    downs = [i for i in range(27) if i // 3 % 3 == 0]
+    for k in range(9):
+        for x in range(size_x):
+            last = (x + 1) * size_y - 1
+            y_send[0, k, x : x + 1, :] = cells[ups[k], last : last + 1, :]
+            first = x * size_y
+            y_send[1, k, x : x + 1, :] = cells[downs[k], first : first + 1, :]
+    edge_copies += [
+        send(y_send.at[0], y_in.at[0], (gx, next_y, gz)),
+        send(y_send.at[1], y_in.at[1], (gx, past_y, gz)),
+    ]
+    for k in range(9):
+        cells[3 * k + 2] = pltpu.roll(cells[3 * k + 2], 1, 1)
+        cells[3 * k] = pltpu.roll(cells[3 * k], LANES - 1, 1)
 
     pieces = []
     for d in range(3):
@@ -501,47 +522,46 @@
     store(vel_out, vel_hbm_out)
     store(disp_out, disp_hbm_out)
 
-    z_copy.wait_recv()
-    column = z_in[...]
+    def fill_lanes(k, side, column, rolled, lanes):
+        if side == 2:
+            above = column if k == 0 else pltpu.roll(column, LANES - k, 1)
+            return jnp.where(
+                lanes == 0, jnp.where(at_bottom, inflow[3 * k + 2], above), rolled
+            )
+        below = pltpu.roll(column, LANES - 1 - k, 1)
+        return jnp.where(
+            lanes == LANES - 1, jnp.where(at_bottom, below, inflow[3 * k]), rolled
+        )
+
+    for copy in edge_copies:
+        copy.wait_recv()
+    column = z_in[0]
     for k in range(9):
-        up, down = 3 * k + 2, 3 * k
-        above = column if k == 0 else pltpu.roll(column, LANES - k, 1)
-        cells[up] = jnp.where(
-            lane == 0, jnp.where(at_bottom, inflow[up], above), pltpu.roll(cells[up], 1, 1)
-        )
-        cells[down] = jnp.where(
-            lane == LANES - 1,
-            jnp.where(at_bottom, pltpu.roll(column, LANES - 1 - k, 1), inflow[down]),
-            pltpu.roll(cells[down], LANES - 1, 1),
-        )
-
-    ups = [i for i in range(27) if i // 3 % 3 == 2]
-    downs = [i for i in range(27) if i // 3 % 3 == 0]
+        for side in (0, 2):
+            i = 3 * k + side
+            cells[i] = fill_lanes(k, side, column, cells[i], lane)
+
+    row = lax.broadcasted_iota(jnp.int32, (size_y, LANES), 0)
+    z_edge[...] = jnp.zeros_like(z_edge)
+    for x in range(size_x):
+        last = (x + 1) * size_y - 1
+        z_edge[0, x : x + 1, :] = z_in[1, last : last + 1, :]
+        z_edge[1, x : x + 1, :] = z_in[2, x * size_y : x * size_y + 1, :]
+    at_front, at_back = gy == 0, gy == columns - 1
     for k in range(9):
-        for x in range(size_x):
-            spot = k * size_x + x
-            last = (x + 1) * size_y - 1
-            y_send[0, spot : spot + 1, :] = cells[ups[k], last : last + 1, :]
-            first = x * size_y
-            y_send[1, spot : spot + 1, :] = cells[downs[k], first : first + 1, :]
-    y_copies = [
-        send(y_send.at[0], y_in.at[0], (gx, lax.rem(gy + 1, columns), gz)),
-        send(y_send.at[1], y_in.at[1], (gx, lax.rem(gy + columns - 1, columns), gz)),
-    ]
-    row = lax.broadcasted_iota(jnp.int32, (size_y, LANES), 0)
-    for copy in y_copies:
-        copy.wait_recv()
-    for k in range(9):
-        for x in range(size_x):
-            spot = k * size_x + x
-            span = slice(x * size_y, (x + 1) * size_y)
-            up, down = ups[k], downs[k]
-            below = jnp.where(gy == 0, inflow[up], y_in[0, spot : spot + 1, :])
-            cells[up, span, :] = jnp.where(row == 0, below, pltpu.roll(cells[up, span, :], 1, 0))
-            above = jnp.where(gy == columns - 1, inflow[down], y_in[1, spot : spot + 1, :])
-            cells[down, span, :] = jnp.where(
-                row == size_y - 1, above, pltpu.roll(cells[down, span, :], size_y - 1, 0)
-            )
+        for way, i in ((0, ups[k]), (1, downs[k])):
+            halo = y_in[way, k]
+            side = i % 3
+            if side == 2:
+                halo = fill_lanes(i // 3, 2, z_edge[way], pltpu.roll(halo, 1, 1), lane8)
+            elif side == 0:
+                halo = fill_lanes(i // 3, 0, z_edge[way], pltpu.roll(halo, LANES - 1, 1), lane8)
+            halo = jnp.where(at_back if way else at_front, inflow[i], halo)
+            for x in range(size_x):
+                span = slice(x * size_y, (x + 1) * size_y)
+                moved = pltpu.roll(cells[i, span, :], size_y - 1 if way else 1, 0)
+                edge = size_y - 1 if way else 0
+                cells[i, span, :] = jnp.where(row == edge, halo[x : x + 1], moved)
 
     tail = plane - size_y
     x_copies = [
@@ -608,7 +628,8 @@
     ranks = columns * layers
     width = -(-3 * points // LANES) * LANES
     assert ranks == 8 and layers == 2 and size_z == LANES and points <= 8 * LANES
-    copies = 2 * (slabs - 1) + 2 * (ranks - 1) + 5
+    assert columns > 2 and size_x <= 8
+    copies = 2 * (slabs - 1) + 2 * (ranks - 1) + 7
     hbm = pl.BlockSpec(memory_space=pltpu.HBM)
     whole = jnp.int32
     full = jnp.float32
@@ -658,9 +679,10 @@
             pltpu.VMEM((8, width), full),
             pltpu.VMEM((3 * plane, LANES), full),
             pltpu.VMEM((plane, LANES), full),
-            pltpu.VMEM((plane, LANES), full),
-            pltpu.VMEM((2, 9 * size_x + 4, LANES), full),
-            pltpu.VMEM((2, 9 * size_x + 4, LANES), full),
+            pltpu.VMEM((3, plane, LANES), full),
+            pltpu.VMEM((2, 9, 8, LANES), full),
+            pltpu.VMEM((2, 9, 8, LANES), full),
+            pltpu.VMEM((2, 8, LANES), full),
             pltpu.VMEM((2, 9, size_y, LANES), full),
             pltpu.SemaphoreType.DMA((13,)),
             pltpu.SemaphoreType.DMA((8,)),

time: 36.2 us -> 34.3 us (0.948)
  Pallas kernels: 34.8 us -> 32.8 us
    pallas_call x1, Pallas kernels: 32.8 us -> 30.8 us  [body(): pl.pallas_call(functools.partial(kernel, (slabs, columns, layers, points,...]
where the time goes in v4:
time: 34.3 us; the launch traced here: 34.1 us
  Pallas kernels  32.8 us (96%)
  between operations  1.29 us (4%)
    pallas_call x1, Pallas kernels, body(): pl.pallas_call(functools.partial(kernel, (slabs, columns, layers, points,...  30.8 us
    pallas_call x1, Pallas kernels, body(): pl.pallas_call(store_kernel, out_shape=tuple((jax.ShapeDtypeStruct(o.shap...  2 us

profile of v4, /device:TPU:0, one launch (start us, length us, event | category | flops | bytes accessed | tf_op | source)
XLA Modules:
  0.0 34.1 jit_solution(13431237130145114725)
XLA Ops:
  1.3 30.8 %shard_map.156 = (f32[27,64,128]{2,1,0:T(8,128)}, f32[192,128]{1,0:T(8,128)}, f32[1,512]{1,0:T(1,128)}, f32[1,512]{1,0:T(1,128)}) custom-call(f32[27,64,128]{2,1,0:T(8,128)} %bitcast.9, f32[27]{0:T(128)} %relax_hbm.1, s32[1,1024]{1,0:T(1,128)} %bitcast.11, s32[3,1024]{1,0:T(4,128)} %offset_hbm.1, f32[64,1024]{1,0:T(8,128)} %weight_hbm.1, ...), custom_call_target="tpu_custom_call" | custom-call | tf_op jit(solution)/shard_map/pallas_call | solution.py:637
  32.1 2.0 %shard_map.157 = (f32[27,64,128]{2,1,0:T(8,128)}, f32[192,128]{1,0:T(8,128)}, f32[1,512]{1,0:T(1,128)}, f32[1,512]{1,0:T(1,128)}) custom-call(f32[27,64,128]{2,1,0:T(8,128)} %get-tuple-element.12.refs_0_, f32[192,128]{1,0:T(8,128)} %get-tuple-element.13.refs_1_, f32[1,512]{1,0:T(1,128)} %get-tuple-element.14.refs_2_, f32[1,512]{1,0:T(1,128)} %get-tuple-element.15.refs_3_), custom_call_target="tpu_custom_call" | custom-call | tf_op jit(solution)/shard_map/pallas_call | solution.py:710

commit v5 on v4

--- a/solution.py
+++ b/solution.py
@@ -216,7 +216,7 @@
             spread[spot, :] = raw
         return 0
 
-    lax.fori_loop(0, plane // 8, moments_of, 0)
+    lax.fori_loop(0, plane // 8, moments_of, 0, unroll=2)
     raw_high, raw_low = halves(spread[...])
     raw_pair[:, :LANES] = raw_high
     raw_pair[:, LANES:] = raw_low
@@ -290,7 +290,7 @@
         ).reshape(8, rows, LANES)
         return 0
 
-    lax.fori_loop(0, capacity // CHUNK, gather, 0)
+    lax.fori_loop(0, capacity // CHUNK, gather, 0, unroll=True)
 
     pl.semaphore_wait(barrier, slabs - 1 + ranks - 1)
 
@@ -397,7 +397,7 @@
         spread[...] += total
         return 0
 
-    lax.fori_loop(0, capacity // CHUNK, scatter, 0)
+    lax.fori_loop(0, capacity // CHUNK, scatter, 0, unroll=True)
     force_out[...] = -spread[...]
     store(force_out, force_hbm_out)
 
@@ -458,7 +458,7 @@
             cells[i, part, :] = pops[i, part, :] + values[i]
         return 0
 
-    lax.fori_loop(0, plane // 8, collide, 0)
+    lax.fori_loop(0, plane // 8, collide, 0, unroll=2)
 
     lane = lax.broadcasted_iota(jnp.int32, (plane, LANES), 1)
     at_bottom = gz == 0

time: 34.3 us -> 32.9 us (0.959)
  Pallas kernels: 32.8 us -> 31.4 us
    pallas_call x1, Pallas kernels: 30.8 us -> 29.4 us  [body(): pl.pallas_call(functools.partial(kernel, (slabs, columns, layers, points,...]
where the time goes in v5:
time: 32.9 us; the launch traced here: 32.7 us
  Pallas kernels  31.4 us (95%)
  between operations  1.29 us (4%)
    pallas_call x1, Pallas kernels, body(): pl.pallas_call(functools.partial(kernel, (slabs, columns, layers, points,...  29.4 us
    pallas_call x1, Pallas kernels, body(): pl.pallas_call(store_kernel, out_shape=tuple((jax.ShapeDtypeStruct(o.shap...  2 us

profile of v5, /device:TPU:0, one launch (start us, length us, event | category | flops | bytes accessed | tf_op | source)
XLA Modules:
  0.0 32.7 jit_solution(11281712033725750662)
XLA Ops:
  1.3 29.4 %shard_map.156 = (f32[27,64,128]{2,1,0:T(8,128)}, f32[192,128]{1,0:T(8,128)}, f32[1,512]{1,0:T(1,128)}, f32[1,512]{1,0:T(1,128)}) custom-call(f32[27,64,128]{2,1,0:T(8,128)} %bitcast.9, f32[27]{0:T(128)} %relax_hbm.1, s32[1,1024]{1,0:T(1,128)} %bitcast.11, s32[3,1024]{1,0:T(4,128)} %offset_hbm.1, f32[64,1024]{1,0:T(8,128)} %weight_hbm.1, ...), custom_call_target="tpu_custom_call" | custom-call | tf_op jit(solution)/shard_map/pallas_call | solution.py:637
  30.7 2.0 %shard_map.157 = (f32[27,64,128]{2,1,0:T(8,128)}, f32[192,128]{1,0:T(8,128)}, f32[1,512]{1,0:T(1,128)}, f32[1,512]{1,0:T(1,128)}) custom-call(f32[27,64,128]{2,1,0:T(8,128)} %get-tuple-element.12.refs_0_, f32[192,128]{1,0:T(8,128)} %get-tuple-element.13.refs_1_, f32[1,512]{1,0:T(1,128)} %get-tuple-element.14.refs_2_, f32[1,512]{1,0:T(1,128)} %get-tuple-element.15.refs_3_), custom_call_target="tpu_custom_call" | custom-call | tf_op jit(solution)/shard_map/pallas_call | solution.py:710
